TPU v7x, 32 devices: a whole 2x2x4 slice. The times are simulated.
32 devices in a mesh: blk: 4 (over z), ep: 8 (over y, x, core).
Axes of the slice: x: 2, y: 2, z: 4, core: 2. Of those that a mesh axis runs over, the one named last changes fastest.
Arguments:
- hidden_in: bfloat16 [16, 1024, 768], P('ep', 'blk'), may hold values from -6 to 6
- cotangent: bfloat16 [16, 1024, 768], P('ep', 'blk'), may hold values from -6 to 6
- query_weight: bfloat16 [768, 768], replicated, may hold values from -0.3125 to 0.3125
- key_weight: bfloat16 [768, 768], replicated, may hold values from -0.3125 to 0.3125
- value_weight: bfloat16 [768, 768], replicated, may hold values from -0.21875 to 0.21875
- output_weight: bfloat16 [768, 768], replicated, may hold values from -0.875 to 0.875
- gain_one: float32 [768], replicated, may hold values from 0.5 to 1.5
- shift_one: float32 [768], replicated, may hold values from -1.75 to 1.75
- gain_two: float32 [768], replicated, may hold values from 0.5 to 1.5
- shift_two: float32 [768], replicated, may hold values from -1.75 to 1.75
- w_router: bfloat16 [768, 4], replicated, may hold values from -0.15625 to 0.15625
- w_inner: bfloat16 [8, 768, 1536], P('ep', None, 'blk'), may hold values from -0.21875 to 0.21875
- w_outer: bfloat16 [8, 1536, 768], P('ep', 'blk'), may hold values from -0.3125 to 0.3125
- expert_ids: int32 [8, 4, 2, 256, 1], P('ep', 'blk'), may hold values from 0 to 3; in each aligned block of 512 rows (0 to 511, 512 to 1023, ..., all dimensions but the last counted through in order) at most 256 rows name the same one
- seq_lengths: int32 [16], P('ep'), may hold values from 1 to 1024, as said below
Outputs:
- output: bfloat16 [16, 1024, 768], P('ep', 'blk')
- grad_hidden: float32 [16, 1024, 768], P('ep', 'blk')
- grad_query: float32 [768, 768], replicated
- grad_key: float32 [768, 768], replicated
- grad_value: float32 [768, 768], replicated
- grad_out: float32 [768, 768], replicated
- grad_gain_one: float32 [768], replicated
- grad_shift_one: float32 [768], replicated
- grad_gain_two: float32 [768], replicated
- grad_shift_two: float32 [768], replicated
- grad_router: float32 [768, 4], replicated
- grad_inner: float32 [8, 768, 1536], P('ep', None, 'blk')
- grad_outer: float32 [8, 1536, 768], P('ep', 'blk')
- balance: float32 [], replicated
Inputs may be any that keep to these rules, and one draw needn't show every extreme that they name: `expert_ids`: each aligned block of 512 rows (the tokens of one device, in the array's order) names one expert at most 256 times. `seq_lengths`: of the 2 sequences held by one index of ep, one has all 1024 tokens.
All inputs are finite; a program needn't handle non-finite values.
Results may differ from a plain program's by a relative error of at most 0.018.
Values may be sent and summed in bfloat16 or wider, within the bound.
A program may use at most 256 MiB of HBM per device.

v0:
```python
import jax
import jax.numpy as jnp
from jax import lax
from jax.sharding import PartitionSpec as P

HEAD = 64


epsilon = 1e-05
balance_weight = 6.0
masked_fill = -1e30
start_max = -1e20


def layer_norm(inputs, norm_gain, norm_shift):
    centered = inputs - jnp.mean(inputs, axis=-1, keepdims=True)
    variance = jnp.mean(centered * centered, axis=-1, keepdims=True)
    return centered * lax.rsqrt(variance + epsilon) * norm_gain + norm_shift


def gelu_exact(values):
    return jax.nn.gelu(values, approximate=False)


def gelu_slope(pre_act, d_act):
    return jax.vjp(gelu_exact, pre_act)[1](d_act)[0]


def split_heads(row_block, head_count):
    return row_block.reshape(
        row_block.shape[0], row_block.shape[1], head_count, row_block.shape[2] // head_count
    )


def keep_running(running, sub_part, first_key):
    return running


def on_device(
    hidden_in,
    cotangent,
    query_weight,
    key_weight,
    value_weight,
    output_weight,
    gain_one,
    shift_one,
    gain_two,
    shift_two,
    w_router,
    w_inner,
    w_outer,
    expert_ids,
    seq_lengths,
):
    seq_count, span_rows, model_width = hidden_in.shape
    tok_count = seq_count * span_rows
    head_count = model_width // HEAD
    scale_factor = HEAD ** (-0.5)
    blocks = lax.axis_size("blk")
    block_index = lax.axis_index("blk")
    ep_count = lax.axis_size("ep")
    experts = w_router.shape[1]
    capacity = max(2, 2 * tok_count // experts)
    f32 = jnp.float32
    bf16 = jnp.bfloat16
    inputs = hidden_in.astype(f32)
    normed_f, norm_one_pull = jax.vjp(layer_norm, inputs, gain_one, shift_one)
    normalized_input = normed_f.astype(bf16)
    query_rows = jnp.einsum(
        "scd,de->sce", normalized_input, query_weight, preferred_element_type=f32
    ).astype(bf16)
    projected_keys = jnp.einsum(
        "scd,de->sce", normalized_input, key_weight, preferred_element_type=f32
    ).astype(bf16)
    projected_values = jnp.einsum(
        "scd,de->sce", normalized_input, value_weight, preferred_element_type=f32
    ).astype(bf16)
    query_heads = split_heads(query_rows, head_count)
    query_places = block_index * span_rows + jnp.arange(span_rows, dtype=jnp.int32)
    last_query = block_index * span_rows + span_rows - 1

    def allowed_pairs(first_key, key_count):
        key_places = first_key + jnp.arange(key_count, dtype=jnp.int32)
        causal = key_places[None, None, :] <= query_places[None, :, None]
        inside = key_places[None, None, :] < seq_lengths[:, None, None]
        return (causal & inside)[:, None, :, :]

    def pieces_of(pieces, first_row, step_fn, running):
        key_count = pieces[0].shape[1]
        sub_part = tuple((piece_rows for piece_rows in pieces))
        running = lax.cond(
            first_row > last_query, keep_running, step_fn, running, sub_part, first_row
        )
        return running

    def forward_step(running, sub_part, first_key):
        run_max, run_sum, run_acc = running
        key_part, value_part = sub_part
        key_count = key_part.shape[1]
        scores = (
            jnp.einsum(
                "sqhe,skhe->shqk",
                query_heads,
                split_heads(key_part, head_count),
                preferred_element_type=f32,
            )
            * scale_factor
        )
        scores = jnp.where(allowed_pairs(first_key, key_count), scores, masked_fill)
        new_max = jnp.maximum(run_max, jnp.max(scores, axis=-1))
        factor = jnp.exp(run_max - new_max)
        prob_rows = jnp.exp(scores - new_max[..., None])
        run_sum = run_sum * factor + jnp.sum(prob_rows, axis=-1)
        product = jnp.einsum(
            "shqk,skhe->sqhe",
            prob_rows.astype(bf16),
            split_heads(value_part, head_count),
            preferred_element_type=f32,
        )
        return (new_max, run_sum, run_acc * jnp.transpose(factor, (0, 2, 1))[..., None] + product)

    head_size = model_width // head_count
    start_state = (
        jnp.full((seq_count, head_count, span_rows), start_max, f32),
        jnp.zeros((seq_count, head_count, span_rows), f32),
        jnp.zeros((seq_count, span_rows, head_count, head_size), f32),
    )
    key_all, value_all = (
        lax.all_gather(projected_keys, "blk", axis=1, tiled=True),
        lax.all_gather(projected_values, "blk", axis=1, tiled=True),
    )
    running = start_state
    for piece_index in range(blocks):
        sub_pieces = (
            key_all[:, piece_index * span_rows : (piece_index + 1) * span_rows],
            value_all[:, piece_index * span_rows : (piece_index + 1) * span_rows],
        )
        running = pieces_of(sub_pieces, piece_index * span_rows, forward_step, running)
    run_max, run_sum, run_acc = running
    log_total = run_max + jnp.log(run_sum)
    attended_f = run_acc / jnp.transpose(run_sum, (0, 2, 1))[..., None]
    attended_rows = attended_f.reshape(seq_count, span_rows, model_width).astype(bf16)
    branch_output = jnp.einsum(
        "scd,de->sce", attended_rows, output_weight, preferred_element_type=f32
    )
    middle = inputs + branch_output
    middle_flat = middle.reshape(tok_count, model_width)
    normed_two_f, norm_two_pull = jax.vjp(layer_norm, middle_flat, gain_two, shift_two)
    flat_rows = normed_two_f.astype(bf16)
    logits = jnp.dot(flat_rows, w_router, preferred_element_type=f32)
    token_experts = expert_ids.reshape(tok_count)
    onehot = token_experts[:, None] == jnp.arange(experts, dtype=jnp.int32)[None, :]
    onehot_f = onehot.astype(f32)
    gate_values = jax.nn.sigmoid(jnp.sum(logits * onehot_f, axis=1))
    valid_rows = (query_places[None, :] < seq_lengths[:, None]).astype(f32).reshape(tok_count)
    counts = lax.psum(jnp.sum(onehot_f * valid_rows[:, None], axis=0), ("blk", "ep"))
    mean_load = jnp.sum(counts) / experts
    load_ratio = (counts - mean_load) / mean_load
    onehot_int = onehot.astype(jnp.int32)
    slot_ranks = jnp.sum(jnp.cumsum(onehot_int, axis=0) * onehot_int, axis=1) - 1
    slot_rows = token_experts * capacity + slot_ranks

    def both_halves(slot_table):
        paired = jnp.broadcast_to(
            slot_table.reshape(experts, 1, capacity, model_width),
            (experts, 2, capacity, model_width),
        )
        return paired.reshape(ep_count, capacity, model_width)

    def join_halves(returned_rows):
        return jnp.sum(returned_rows.reshape(experts, 2, capacity, model_width), axis=1).reshape(
            experts * capacity, model_width
        )

    send_rows = jnp.zeros((experts * capacity, model_width), bf16).at[slot_rows].set(flat_rows)
    received = lax.all_to_all(both_halves(send_rows), "ep", split_axis=0, concat_axis=0, tiled=True)
    expert_rows = received.reshape(-1, model_width)
    inner_weight = w_inner[0]
    outer_weight = w_outer[0]
    pre_all = jnp.dot(
        lax.all_gather(expert_rows, "blk", axis=0, tiled=True),
        inner_weight,
        preferred_element_type=f32,
    )
    activation = gelu_exact(pre_all).astype(bf16)
    act_part = activation
    produced = lax.psum_scatter(
        jnp.dot(act_part, outer_weight, preferred_element_type=f32).astype(jnp.bfloat16),
        "blk",
        scatter_dimension=0,
        tiled=True,
    ).astype(jnp.float32)
    returned = lax.all_to_all(
        produced.reshape(ep_count, capacity, model_width).astype(jnp.bfloat16),
        "ep",
        split_axis=0,
        concat_axis=0,
        tiled=True,
    ).astype(jnp.float32)
    expert_out = join_halves(returned).astype(bf16)[slot_rows]
    scale_rows = valid_rows * gate_values
    output_f = middle_flat + scale_rows[:, None] * expert_out.astype(f32)
    output = output_f.reshape(seq_count, span_rows, model_width).astype(bf16)
    ratio_rows = jnp.sum(onehot_f * load_ratio[None, :], axis=1)
    local_balance = jnp.sum(scale_rows * ratio_rows)
    grad_flat = cotangent.astype(f32).reshape(tok_count, model_width)
    d_expert = (scale_rows[:, None] * grad_flat).astype(bf16)
    d_gate = valid_rows * (
        jnp.sum(grad_flat * expert_out.astype(f32), axis=1) + balance_weight * ratio_rows
    )
    d_logits = (onehot_f * (d_gate * gate_values * (1.0 - gate_values))[:, None]).astype(bf16)
    grad_router = jnp.einsum("td,te->de", flat_rows, d_logits, preferred_element_type=f32)
    d_router_rows = jnp.einsum("te,de->td", d_logits, w_router, preferred_element_type=f32)
    d_send = jnp.zeros((experts * capacity, model_width), bf16).at[slot_rows].set(d_expert)
    d_received = lax.all_to_all(
        both_halves(d_send), "ep", split_axis=0, concat_axis=0, tiled=True
    ).reshape(-1, model_width)
    d_piece = lax.all_gather(d_received, "blk", axis=0, tiled=True)
    row_piece = lax.all_gather(expert_rows, "blk", axis=0, tiled=True)
    act_part = activation
    grad_out_acc = jnp.einsum("rf,rd->fd", act_part, d_piece, preferred_element_type=f32)
    d_act = jnp.einsum("rd,fd->rf", d_piece, outer_weight, preferred_element_type=f32)
    d_pre = gelu_slope(pre_all, d_act).astype(bf16)
    grad_in_acc = jnp.einsum("rd,rf->df", row_piece, d_pre, preferred_element_type=f32)
    d_rows = lax.psum_scatter(
        jnp.einsum("rf,df->rd", d_pre, inner_weight, preferred_element_type=f32).astype(
            jnp.bfloat16
        ),
        "blk",
        scatter_dimension=0,
        tiled=True,
    ).astype(jnp.float32)
    grad_inner = grad_in_acc[None]
    grad_outer = grad_out_acc[None]
    d_back = lax.all_to_all(
        d_rows.reshape(ep_count, capacity, model_width).astype(jnp.bfloat16),
        "ep",
        split_axis=0,
        concat_axis=0,
        tiled=True,
    ).astype(jnp.float32)
    d_expert_rows = join_halves(d_back).astype(bf16)[slot_rows].astype(f32)
    d_middle_norm, grad_gain_two, grad_shift_two = norm_two_pull(d_expert_rows + d_router_rows)
    d_middle = (grad_flat + d_middle_norm).reshape(seq_count, span_rows, model_width)
    d_branch = d_middle.astype(bf16)
    grad_out = jnp.einsum("scd,sce->de", attended_rows, d_branch, preferred_element_type=f32)
    d_attended = jnp.einsum(
        "sce,de->scd", d_branch, output_weight, preferred_element_type=f32
    ).astype(bf16)
    d_att_heads = split_heads(d_attended, head_count)
    row_delta = jnp.transpose(jnp.sum(d_att_heads.astype(f32) * attended_f, axis=-1), (0, 2, 1))

    def backward_step(running, sub_part, first_key):
        d_query_acc, key_grads = running
        key_part, value_part = sub_part
        key_count = key_part.shape[1]
        key_heads = split_heads(key_part, head_count)
        value_heads = split_heads(value_part, head_count)
        scores = (
            jnp.einsum("sqhe,skhe->shqk", query_heads, key_heads, preferred_element_type=f32)
            * scale_factor
        )
        prob_rows = jnp.where(
            allowed_pairs(first_key, key_count), jnp.exp(scores - log_total[..., None]), 0.0
        )
        d_value = jnp.einsum(
            "shqk,sqhe->skhe", prob_rows.astype(bf16), d_att_heads, preferred_element_type=f32
        )
        d_probs = jnp.einsum(
            "sqhe,skhe->shqk", d_att_heads, value_heads, preferred_element_type=f32
        )
        d_scores = (prob_rows * (d_probs - row_delta[..., None])).astype(bf16)
        d_query_acc = (
            d_query_acc
            + jnp.einsum("shqk,skhe->sqhe", d_scores, key_heads, preferred_element_type=f32)
            * scale_factor
        )
        d_key = (
            jnp.einsum("shqk,sqhe->skhe", d_scores, query_heads, preferred_element_type=f32)
            * scale_factor
        )
        joined = jnp.concatenate(
            [
                d_key.reshape(seq_count, key_count, model_width),
                d_value.reshape(seq_count, key_count, model_width),
            ],
            axis=2,
        )
        key_grads = lax.dynamic_update_slice_in_dim(key_grads, joined, first_key, 1)
        return (d_query_acc, key_grads)

    back_start = (
        jnp.zeros((seq_count, span_rows, head_count, head_size), f32),
        jnp.zeros((seq_count, span_rows * blocks, 2 * model_width), f32),
    )
    running = back_start
    for piece_index in range(blocks):
        sub_pieces = (
            key_all[:, piece_index * span_rows : (piece_index + 1) * span_rows],
            value_all[:, piece_index * span_rows : (piece_index + 1) * span_rows],
        )
        running = pieces_of(sub_pieces, piece_index * span_rows, backward_step, running)
    d_query_acc, key_grads = running
    key_sums = lax.psum_scatter(
        key_grads.astype(jnp.bfloat16), "blk", scatter_dimension=1, tiled=True
    ).astype(jnp.float32)
    d_queries = d_query_acc.reshape(seq_count, span_rows, model_width).astype(bf16)
    d_keys = key_sums[:, :, :model_width].astype(bf16)
    d_values = key_sums[:, :, model_width:].astype(bf16)
    grad_query = jnp.einsum("scd,sce->de", normalized_input, d_queries, preferred_element_type=f32)
    grad_key = jnp.einsum("scd,sce->de", normalized_input, d_keys, preferred_element_type=f32)
    grad_value = jnp.einsum("scd,sce->de", normalized_input, d_values, preferred_element_type=f32)
    d_normed = (
        jnp.einsum("sce,de->scd", d_queries, query_weight, preferred_element_type=f32)
        + jnp.einsum("sce,de->scd", d_keys, key_weight, preferred_element_type=f32)
        + jnp.einsum("sce,de->scd", d_values, value_weight, preferred_element_type=f32)
    )
    d_input_norm, grad_gain_one, grad_shift_one = norm_one_pull(d_normed)
    grad_hidden = d_middle + d_input_norm
    summed = lax.psum(
        (
            grad_query,
            grad_key,
            grad_value,
            grad_out,
            grad_gain_one,
            grad_shift_one,
            grad_gain_two,
            grad_shift_two,
            grad_router,
            local_balance,
        ),
        ("blk", "ep"),
    )
    balance = summed[9] / jnp.sum(counts)
    return (
        output,
        grad_hidden,
        summed[0],
        summed[1],
        summed[2],
        summed[3],
        summed[4],
        summed[5],
        summed[6],
        summed[7],
        summed[8],
        grad_inner,
        grad_outer,
        balance,
    )


def solution(mesh):
    return jax.shard_map(
        on_device,
        mesh=mesh,
        in_specs=(
            P("ep", "blk", None),
            P("ep", "blk", None),
            P(),
            P(),
            P(),
            P(),
            P(),
            P(),
            P(),
            P(),
            P(),
            P("ep", None, "blk"),
            P("ep", "blk", None),
            P("ep", "blk", None, None, None),
            P("ep"),
        ),
        out_specs=(
            P("ep", "blk", None),
            P("ep", "blk", None),
            P(),
            P(),
            P(),
            P(),
            P(),
            P(),
            P(),
            P(),
            P(),
            P("ep", None, "blk"),
            P("ep", "blk", None),
            P(),
        ),
        check_vma=False,
    )
```

profile of v0, /device:TPU:9, one launch (start us, length us, event | category | flops | bytes accessed | tf_op | source)
XLA Modules:
  0.0 1655.2 jit_solution(17091034130465651898)
XLA Ops:
  20.8 54.8 %all-gather.7.cloned.1.call-done = bf16[2,1024,768]{2,1,0:T(8,128)(2,1)} async-done(((bf16[2,256,768]{2,1,0:T(8,128)(2,1)}), bf16[2,1024,768]{2,1,0:T(8,128)(2,1)}) %all-gather.7.cloned.1.call-update) | async-done | bytes 3145744 | tf_op jit(solution)/shard_map/all_gather | solution.py:131
  75.6 3.3 fusion.169
  79.0 61.1 %all-gather.5.cloned.1.call-done = bf16[2,1024,768]{2,1,0:T(8,128)(2,1)} async-done(((bf16[2,256,768]{2,1,0:T(8,128)(2,1)}), bf16[2,1024,768]{2,1,0:T(8,128)(2,1)}) %all-gather.5.cloned.1.call-update) | async-done | bytes 3145744 | tf_op jit(solution)/shard_map/all_gather | solution.py:130
  140.0 3.6 fusion.170
  143.6 13.5 conditional.15
  152.5 4.5 bitcast_add_fusion
  157.1 21.6 %conditional.16 = (f32[2,12,256]{2,1,0:T(8,128)S(1)}, f32[2,12,256]{2,1,0:T(8,128)}, f32[2,256,12,64]{1,3,2,0:T(8,128)S(1)}) conditional(s32[]{:T(128)} %convert_element_type.183, (s32[256]{0:T(256)S(1)}, s32[2]{0:T(128)S(1)}, bf16[2,256,768]{2,1,0:T(8,128)(2,1)}, bf16[2,256,12,64]{1,3,2,0:T(8,128)(2,1)S(1)}, f32[2,12,256]{2,1,0:T(8,128)}, ...), branch_computations={%region_6.9_spmd, %region_9.10_spmd} | conditional | flops 420956928 | bytes 29349008 | solution.py:92
  160.6 5.0 fusion.15
  168.5 4.7 bitcast_add_fusion.1
  173.2 4.1 fusion.17
  185.8 3.8 scatter_custom_fusion
  191.2 40.9 %all_to_all.20 = bf16[8,256,768]{2,1,0:T(8,128)(2,1)} all-to-all(bf16[8,256,768]{2,1,0:T(8,128)(2,1)S(1)} %bitcast.264), channel_id=1, replica_groups=mesh['blk'=4,'ep'=8] {'ep'}, dimensions={0} | all-to-all | bytes 6291456 | tf_op jit(solution)/shard_map/all_to_all | solution.py:177
  232.4 87.7 %psum.77 = f32[4]{0:T(128)S(1)} all-reduce(f32[4]{0:T(128)S(1)} %select_reduce_fusion.1), channel_id=1, replica_groups=mesh['blk'=4,'ep'=8] {'blk','ep'}, use_global_device_ids=true, to_apply=%region_32.33 | all-reduce | flops 4 | bytes 32 | tf_op jit(solution)/shard_map/psum | solution.py:157
  326.5 41.0 %all_to_all.21 = bf16[8,256,768]{2,1,0:T(8,128)(2,1)} all-to-all(bf16[8,256,768]{2,1,0:T(8,128)(2,1)S(1)} %bitcast.265), channel_id=1, replica_groups=mesh['blk'=4,'ep'=8] {'ep'}, dimensions={0} | all-to-all | bytes 6291456 | tf_op jit(solution)/shard_map/all_to_all | solution.py:216
  367.8 117.3 %all-gather.9.cloned.1.call-done = bf16[8192,768]{1,0:T(8,128)(2,1)} async-done(((bf16[2048,768]{1,0:T(8,128)(2,1)}), bf16[8192,768]{1,0:T(8,128)(2,1)}) %all-gather.9.cloned.1.call-update) | async-done | bytes 12582928 | tf_op jit(solution)/shard_map/all_gather | solution.py:182
  485.1 36.2 %multiply_convert_fusion.4 = (bf16[8192,384]{1,0:T(8,128)(2,1)}, f32[8192,384]{1,0:T(8,128)}, f32[8192,384]{1,0:T(8,128)}) fusion(bf16[8192,768]{1,0:T(8,128)(2,1)} %all-gather.9.cloned.1.call-done, bf16[1,768,384]{2,1,0:T(8,128)(2,1)S(1)} %copy-done.94), kind=kOutput, calls=%fused_computation.160 | convolution fusion | flops 5036310528 | bytes 44630016 | tf_op jit(solution)/shard_map/dot_general | solution.py:181
  521.3 181.7 %all-gather.11.cloned.1.call-done = bf16[8192,768]{1,0:T(8,128)(2,1)} async-done(((bf16[2048,768]{1,0:T(8,128)(2,1)}), bf16[8192,768]{1,0:T(8,128)(2,1)}) %all-gather.11.cloned.1.call-update) | async-done | bytes 12582928 | tf_op jit(solution)/shard_map/all_gather | solution.py:219
  703.0 19.6 %add_convert_fusion = bf16[8192,384]{1,0:T(8,128)(2,1)} fusion(f32[8192,384]{1,0:T(8,128)} %get-tuple-element.501, f32[8192,384]{1,0:T(8,128)} %get-tuple-element.522, bf16[8192,768]{1,0:T(8,128)(2,1)} %all-gather.11.cloned.1.call-done, bf16[1,384,768]{2,1,0:T(8,128)(2,1)S(1)} %copy-done.95), kind=kOutput, calls=%fused_computation.159 | convolution fusion | flops 4875878400 | bytes 44630016 | tf_op jit(solution)/shard_map/rd,fd->rf/dot_general | solution.py:223
  722.7 12.1 convolution_convert_fusion
  734.8 11.9 convolution_convert_fusion.1
  746.7 201.1 %reduce-scatter.6.cloned.1.call-done = bf16[2048,768]{1,0:T(8,128)(2,1)} async-done(((bf16[8192,768]{1,0:T(8,128)(2,1)}), bf16[2048,768]{1,0:T(8,128)(2,1)}) %reduce-scatter.6.cloned.1.call-update) | async-done | bytes 3145744 | tf_op jit(solution)/shard_map/reduce_scatter | solution.py:226
  947.8 5.0 all-to-all-start.3
  952.8 210.2 %reduce-scatter.4.cloned.1.call-done = bf16[2048,768]{1,0:T(8,128)(2,1)} async-done(((bf16[8192,768]{1,0:T(8,128)(2,1)}), bf16[2048,768]{1,0:T(8,128)(2,1)}) %reduce-scatter.4.cloned.1.call-update) | async-done | bytes 3145744 | tf_op jit(solution)/shard_map/reduce_scatter | solution.py:188
  1163.0 5.0 all-to-all-start.1
  1170.3 3.1 gather_fusion.1
  1173.4 28.9 %all-to-all-done.1 = bf16[8,256,768]{2,1,0:T(8,128)(2,1)} async-done(((bf16[8,256,768]{2,1,0:T(8,128)(2,1)}), bf16[8,256,768]{2,1,0:T(8,128)(2,1)}, u32[]{:S(2)}, u32[]{:S(2)}) %all-to-all-start.1) | async-done | bytes 3145760 | tf_op jit(solution)/shard_map/all_to_all | solution.py:194
  1202.3 4.0 bitcast_reduce_fusion.1
  1206.3 5.0 gather_fusion
  1224.4 22.4 %conditional.19 = (f32[2,256,12,64]{1,3,2,0:T(8,128)S(1)}, bf16[2,1024,1536]{1,2,0:T(8,128)(2,1)}) conditional(s32[]{:T(128)} %convert_element_type.184, (s32[256]{0:T(256)S(1)}, s32[2]{0:T(128)S(1)}, bf16[2,256,768]{2,1,0:T(8,128)(2,1)}, bf16[2,256,12,64]{1,3,2,0:T(8,128)(2,1)S(1)}, f32[2,12,256]{2,1,0:T(8,128)}, ...), branch_computations={%region_38.39_spmd, %region_39.40_spmd} | conditional | flops 1045758464 | bytes 61778112 | solution.py:92
  1225.8 3.7 fusion.172
  1230.8 4.6 multiply_convert_fusion
  1236.6 3.8 fusion.44
  1240.4 5.3 select_maximum_fusion
  1246.8 22.8 %conditional.20 = ((f32[2,256,12,64]{1,3,2,0:T(8,128)S(1)}, bf16[2,1024,1536]{1,2,0:T(8,128)(2,1)})) conditional(s32[]{:T(128)} %convert_element_type.183, (s32[256]{0:T(256)S(1)}, s32[2]{0:T(128)S(1)}, bf16[2,256,768]{2,1,0:T(8,128)(2,1)}, bf16[2,256,12,64]{1,3,2,0:T(8,128)(2,1)S(1)}, f32[2,12,256]{2,1,0:T(8,128)}, ...), branch_computations={%region_40.41_spmd, %region_41.42_spmd} | conditional | flops 1027277568 | bytes 52343952 | solution.py:92
  1249.1 4.9 fusion.173
  1257.1 5.0 multiply_convert_fusion.1
  1263.2 3.8 fusion.53
  1270.6 8.6 copy.93
  1282.1 3.3 convolution_bitcast_fusion
  1285.5 3.6 convolution_bitcast_fusion.3
  1289.1 148.5 %reduce-scatter.8.cloned.1.call-done = bf16[2,256,1536]{2,1,0:T(8,128)(2,1)} async-done(((bf16[2,1024,1536]{2,1,0:T(8,128)(2,1)}), bf16[2,256,1536]{2,1,0:T(8,128)(2,1)}) %reduce-scatter.8.cloned.1.call-update) | async-done | bytes 1572880 | tf_op jit(solution)/shard_map/reduce_scatter | solution.py:305
  1437.6 3.7 convolution_bitcast_fusion.1
  1443.7 12.5 convolution_bitcast_fusion.5
  1456.2 13.1 convolution_bitcast_fusion.4
  1478.4 41.1 %all-reduce.1 = (f32[768]{0:T(1024)}, f32[768]{0:T(1024)}, f32[768]{0:T(1024)}, f32[768]{0:T(1024)}, f32[768,4]{0,1:T(4,128)}, /*index=5*/f32[]{:T(128)}) all-reduce(f32[768]{0:T(1024)} %get-tuple-element.470, f32[768]{0:T(1024)} %get-tuple-element.473, f32[768]{0:T(1024)} %get-tuple-element.468, ...), channel_id=1, replica_groups=mesh['blk'=4,'ep'=8] {'blk','ep'}, use_global_device_ids=true, to_apply=%region_54.55 | all-reduce | flops 6145 | bytes 49160 | tf_op jit(solution)/shard_map/psum | solution.py:321
  1521.5 3.1 add_add_fusion.2
  1524.6 112.5 %all-reduce.5.cloned.1.call-done = (f32[768,768]{1,0:T(8,128)}, f32[768,768]{1,0:T(8,128)}, f32[768,768]{1,0:T(8,128)}, f32[768,768]{1,0:T(8,128)}) async-done(((f32[768,768]{1,0:T(8,128)}, f32[768,768]{1,0:T(8,128)}, f32[768,768]{1,0:T(8,128)}, f32[768,768]{1,0:T(8,128)}), (f32[768,768]{1,0:T(8,128)}, f32[768,768]{1,0:T(8,128)}, f32[768,768]{1,0:T(8,128)}, ...) | async-done | bytes 9437200 | tf_op jit(solution)/shard_map/psum | solution.py:321
  1637.0 3.4 copy.160
  (282 shorter events, 98.8 us)
Async XLA Ops:
  7.2 68.5 %all-gather.7.cloned.1.call-start = ((), (), s32[]{:S(2)}) async-start(), calls=%async_computation.8 | async-start | bytes 3932160 | tf_op jit(solution)/shard_map/all_gather | solution.py:131
  8.6 7.9 copy-start.61
  10.2 6.3 copy-start.80
  10.2 6.3 copy-start.78
  13.3 126.7 %all-gather.5.cloned.1.call-start = ((), (), s32[]{:S(2)}) async-start(), calls=%async_computation.7 | async-start | bytes 3932160 | tf_op jit(solution)/shard_map/all_gather | solution.py:130
  16.5 468.7 %all-gather.9.cloned.1.call-start = ((), (), s32[]{:S(2)}) async-start(), calls=%async_computation.9 | async-start | bytes 15728640 | tf_op jit(solution)/shard_map/all_gather | solution.py:182
  19.0 159.7 %copy-start.1 = (bf16[2,256,768]{1,2,0:T(8,128)(2,1)}, bf16[2,256,768]{1,2,0:T(8,128)(2,1)S(1)}, u32[]{:S(2)}) copy-start(bf16[2,256,768]{1,2,0:T(8,128)(2,1)S(1)} %copy.73) | copy-start | bytes 2359300
  20.7 211.5 %copy-start.59 = (s32[256]{0:T(256)}, s32[256]{0:T(256)S(1)}, u32[]{:S(2)}) copy-start(s32[256]{0:T(256)S(1)} %iota_add_fusion.6) | copy-start | bytes 3076
  79.0 64.6 %copy-start.18 = (bf16[2,256,768]{2,1,0:T(8,128)(2,1)}, bf16[2,256,768]{2,1,0:T(8,128)(2,1)S(1)}, u32[]{:S(2)}) copy-start(bf16[2,256,768]{2,1,0:T(8,128)(2,1)S(1)} %get-tuple-element.513) | copy-start | bytes 2359300
  79.0 64.6 %copy-start.71 = (s32[2]{0:T(128)S(1)}, s32[2]{0:T(128)}, u32[]{:S(2)}) copy-start(s32[2]{0:T(128)} %param.45) | copy-start | bytes 28
  160.6 5.0 copy-start.48
  185.3 5.8 copy-start.67
  185.3 5.8 copy-start.69
  185.7 135.7 %copy-start.20 = (bf16[512,768]{1,0:T(8,128)(2,1)}, bf16[512,768]{1,0:T(8,128)(2,1)S(1)}, u32[]{:S(2)}) copy-start(bf16[512,768]{1,0:T(8,128)(2,1)S(1)} %add_convert_fusion.1) | copy-start | bytes 2359300
  232.1 89.4 %copy-start.77 = (bf16[768,4]{0,1:T(4,128)(2,1)S(1)}, bf16[768,4]{0,1:T(4,128)(2,1)}, u32[]{:S(2)}) copy-start(bf16[768,4]{0,1:T(4,128)(2,1)} %param.41) | copy-start | bytes 18436
  232.1 91.0 %copy-start.15 = (bf16[2,256,768]{2,1,0:T(8,128)(2,1)S(1)}, bf16[2,256,768]{2,1,0:T(8,128)(2,1)}, u32[]{:S(2)}) copy-start(bf16[2,256,768]{2,1,0:T(8,128)(2,1)} %param.32) | copy-start | bytes 2359300
  232.1 470.9 %all-gather.11.cloned.1.call-start = ((), (), s32[]{:S(2)}) async-start(), calls=%async_computation.11 | async-start | bytes 15728640 | tf_op jit(solution)/shard_map/all_gather | solution.py:219
  232.3 94.2 %copy-start.89 = (pred[512]{0:T(512)(128)(4,1)}, pred[512]{0:T(512)(128)(4,1)S(1)}, u32[]{:S(2)}) copy-start(pred[512]{0:T(512)(128)(4,1)S(1)} %lt.213) | copy-start | bytes 1540
  367.6 117.6 %copy-start.94 = (bf16[1,768,384]{2,1,0:T(8,128)(2,1)S(1)}, bf16[1,768,384]{2,1,0:T(8,128)(2,1)}, u32[]{:S(2)}) copy-start(bf16[1,768,384]{2,1,0:T(8,128)(2,1)} %param.42) | copy-start | bytes 1769476
  367.6 335.5 %copy-start.95 = (bf16[1,384,768]{2,1,0:T(8,128)(2,1)S(1)}, bf16[1,384,768]{2,1,0:T(8,128)(2,1)}, u32[]{:S(2)}) copy-start(bf16[1,384,768]{2,1,0:T(8,128)(2,1)} %param.43) | copy-start | bytes 1769476
  367.6 580.2 %reduce-scatter.6.cloned.1.call-start = ((), (), s32[]{:S(2)}) async-start(), calls=%async_computation.12 | async-start | bytes 15728640 | tf_op jit(solution)/shard_map/reduce_scatter | solution.py:226
  734.7 428.2 %reduce-scatter.4.cloned.1.call-start = ((), (), s32[]{:S(2)}) async-start(), calls=%async_computation.10 | async-start | bytes 15728640 | tf_op jit(solution)/shard_map/reduce_scatter | solution.py:188
  947.8 215.2 %all-to-all-start.3 = ((bf16[8,256,768]{2,1,0:T(8,128)(2,1)}), bf16[8,256,768]{2,1,0:T(8,128)(2,1)}, u32[]{:S(2)}, u32[]{:S(2)}) async-start(bf16[8,256,768]{2,1,0:T(8,128)(2,1)} %bitcast.281), calls=%async_computation.5 | async-start | bytes 6291456 | tf_op jit(solution)/shard_map/all_to_all | solution.py:236
  1163.0 39.4 %all-to-all-start.1 = ((bf16[8,256,768]{2,1,0:T(8,128)(2,1)}), bf16[8,256,768]{2,1,0:T(8,128)(2,1)}, u32[]{:S(2)}, u32[]{:S(2)}) async-start(bf16[8,256,768]{2,1,0:T(8,128)(2,1)} %bitcast.280), calls=%async_computation.2 | async-start | bytes 6291456 | tf_op jit(solution)/shard_map/all_to_all | solution.py:194
  1167.9 269.6 %reduce-scatter.8.cloned.1.call-start = ((), (), s32[]{:S(2)}) async-start(), calls=%async_computation.13 | async-start | bytes 7864320 | tf_op jit(solution)/shard_map/reduce_scatter | solution.py:305
  1167.9 5.5 copy-start.85
  1206.3 5.0 copy-start.16
  1206.3 7.2 copy-start.7
  1206.3 7.2 copy-start.54
  1206.3 7.2 copy-start.66
  1206.3 7.2 copy-start.68
  1206.3 7.2 copy-start.70
  1211.3 4.9 copy-start.83
  1217.1 5.2 copy-start.5
  1218.3 6.1 copy-start.2
  1218.3 6.1 copy-start.60
  1218.3 6.1 copy-start.72
  1240.4 5.3 copy-start.27
  1279.3 6.2 copy-start.11
  1279.3 6.1 copy-start.62
  1279.3 6.1 copy-start.64
  1279.3 357.7 %all-reduce.5.cloned.1.call-start = ((), (), s32[]{:S(2)}) async-start(), calls=%async_computation.14 | async-start | bytes 18874368 | tf_op jit(solution)/shard_map/psum | solution.py:321
  1285.5 152.1 %copy-start.79 = (f32[2,256]{1,0:T(2,128)S(1)}, f32[2,256]{1,0:T(2,128)}, u32[]{:S(2)}) copy-start(f32[2,256]{1,0:T(2,128)} %copy-done.78) | copy-start | bytes 6148
  1456.2 13.1 copy-start.21
  1456.2 13.1 copy-start.87
  1456.2 13.9 copy-start.8
  1456.2 13.9 copy-start.22
  1456.2 13.9 copy-start.88
  (41 other events, 107.6 us)
Sparse Core Ops, SparseCore 0:
  13.4 62.2 all-gather.6
  77.8 62.1 all-gather.4
  232.2 252.8 all-gather.8
  486.5 216.4 all-gather.10
  734.9 212.8 reduce-scatter.5
  950.0 212.8 reduce-scatter.3
  1279.4 158.0 reduce-scatter.7
  1444.4 192.6 all-reduce.4
where the time goes:
time: 1670 us; the launch traced here: 1660 us
  waiting for transfers between devices  1120 us (67%)
  blocking collectives  211 us (13%)
  matrix products  185 us (11%)
  local copies, waits for them, and re-layouts  64.6 us (4%)
  other arithmetic  48.9 us (3%)
  between operations  18.3 us (1%)
    reduce_scatter x1, waiting for transfers between devices, on_device(): lax.psum_scatter(jnp.dot(act_part, outer_weight, preferred_element_type=f...  210 us
    reduce_scatter x1, waiting for transfers between devices, on_device(): lax.psum_scatter(jnp.einsum('rf,df->rd', d_pre, inner_weight, preferred_e...  201 us
    all_gather x1, waiting for transfers between devices, on_device(): d_piece = lax.all_gather(d_received, 'blk', axis=0, tiled=True)  182 us
    reduce_scatter x1, waiting for transfers between devices, on_device(): lax.psum_scatter(key_grads.astype(jnp.bfloat16), 'blk', scatter_dimension...  148 us
    all_gather x1, waiting for transfers between devices, on_device(): lax.all_gather(expert_rows, 'blk', axis=0, tiled=True)  117 us
    psum x1, waiting for transfers between devices, on_device(): lax.psum((grad_query, grad_key, grad_value, grad_out, grad_gain_one, grad...  112 us
    psum x1, blocking collectives, on_device(): lax.psum(jnp.sum(onehot_f * valid_rows[:, None], axis=0), ('blk', 'ep'))  87.7 us
    all_gather x1, waiting for transfers between devices, on_device(): lax.all_gather(projected_keys, 'blk', axis=1, tiled=True)  61.1 us
  transfers between devices with their start and end apart: 10, of which 9 were waited for; matrix products, arithmetic and copies ran while one was open for 7% of the time, Pallas kernels for 0%

commit v1 on v0

v1 whole, which is shorter than its diff:
```python
import functools

import jax
import jax.numpy as jnp
from jax import lax
from jax.experimental import pallas as pl
from jax.experimental.pallas import tpu as pltpu
from jax.sharding import PartitionSpec as P

HEAD = 64
MESH = pl.DeviceIdType.MESH
ANY = pl.BlockSpec(memory_space=pl.ANY)
VMEM = pl.BlockSpec(memory_space=pltpu.VMEM)
SMEM = pl.BlockSpec(memory_space=pltpu.SMEM)
DMA = pltpu.SemaphoreType.DMA
f32 = jnp.float32
bf16 = jnp.bfloat16

epsilon = 1e-05
balance_weight = 6.0
masked_fill = -1e30
VMEM_BYTES = 50 * 1024 * 1024


def dot(a, b):
    return lax.dot_general(a, b, (((1,), (0,)), ((), ())), preferred_element_type=f32)


def dot_nt(a, b):
    return lax.dot_general(a, b, (((1,), (1,)), ((), ())), preferred_element_type=f32)


def dot_tn(a, b):
    return lax.dot_general(a, b, (((0,), (0,)), ((), ())), preferred_element_type=f32)


def place():
    z = lax.axis_index("blk")
    e = lax.axis_index("ep")
    c = lax.rem(e, 2)
    return z, e, c, e - c


def remote(src, dst, send_sem, recv_sem, z, e):
    return pltpu.make_async_remote_copy(
        src, dst, send_sem, recv_sem, device_id=(z, e), device_id_type=MESH
    )


def greet(partners):
    barrier = pltpu.get_barrier_semaphore()
    for z, e in partners:
        pl.semaphore_signal(barrier, inc=1, device_id=(z, e), device_id_type=MESH)
    pl.semaphore_wait(barrier, len(partners))


def column_partners(blocks, z, c, base):
    found = [(z, base + 1 - c)]
    for step in range(1, blocks):
        for k in range(2):
            found.append((lax.rem(z + step, blocks), base + k))
    return found


def params(collective_id):
    return pltpu.CompilerParams(
        collective_id=collective_id, has_side_effects=True, vmem_limit_bytes=VMEM_BYTES
    )


def normed_exchange(normed, blocks):
    seqs, span, width = normed.shape
    half = span // 2

    def kernel(n_ref, x_ref, loc_sem, send_sem, recv_sem, fsend_sem, frecv_sem):
        z, e, c, base = place()
        seq_core = z // 2
        greet(column_partners(blocks, z, c, base))

        def outgoing(s, k):
            return remote(
                n_ref.at[s, k], x_ref.at[z, k], send_sem.at[s, k], recv_sem.at[z], 2 * c + s, base + k
            )

        def own(s, k):
            return pltpu.make_async_copy(n_ref.at[s, k], x_ref.at[z, k], loc_sem)

        for s in range(seqs):
            for k in range(2):
                to_self = (2 * c + s == z) & (c == k)

                @pl.when(to_self)
                def _():
                    own(s, k).start()

                @pl.when(jnp.logical_not(to_self))
                def _():
                    outgoing(s, k).start()

        def forward(zs):
            return remote(
                x_ref.at[zs, c], x_ref.at[zs, c], fsend_sem.at[zs], frecv_sem.at[zs], z, base + 1 - c
            )

        for step in range(blocks):
            zs = lax.rem(z + step, blocks)
            if step == 0:

                @pl.when(c == seq_core)
                def _():
                    pltpu.make_async_copy(n_ref.at[0, 0], x_ref.at[z, c], loc_sem).wait()

                @pl.when(c != seq_core)
                def _():
                    remote(n_ref.at[0, 0], x_ref.at[z, c], send_sem.at[0, 0], recv_sem.at[z], z, base).wait_recv()
            else:
                remote(n_ref.at[0, 0], x_ref.at[zs, c], send_sem.at[0, 0], recv_sem.at[zs], z, base).wait_recv()
            forward(zs).start()
        for step in range(blocks):
            zs = lax.rem(z + step, blocks)
            forward(zs).wait_send()
            remote(
                x_ref.at[zs, 1 - c], x_ref.at[zs, 1 - c], fsend_sem.at[zs], frecv_sem.at[zs], z, base + 1 - c
            ).wait_recv()
        for s in range(seqs):
            for k in range(2):

                @pl.when(jnp.logical_not((2 * c + s == z) & (c == k)))
                def _():
                    outgoing(s, k).wait_send()

    return pl.pallas_call(
        kernel,
        name="normed_exchange",
        out_shape=jax.ShapeDtypeStruct((blocks, 2, half, width), bf16),
        in_specs=[ANY],
        out_specs=ANY,
        scratch_shapes=[DMA, DMA((seqs, 2)), DMA((blocks,)), DMA((blocks,)), DMA((blocks,))],
        compiler_params=params(1),
    )(normed.reshape(seqs, 2, half, width)).reshape(blocks * span, width)


def attended_exchange(att, blocks):
    _, span, width = att.shape
    seqs = 2

    def kernel(a_ref, t_ref, loc_sem, send_sem, recv_sem):
        z, e, c, base = place()
        seq_core, seq = z // 2, lax.rem(z, 2)
        greet(column_partners(blocks, z, c, base))

        def outgoing(j):
            return remote(
                a_ref.at[j], t_ref.at[seq, c], send_sem.at[j], recv_sem.at[seq, c], j, base + seq_core
            )

        def own():
            return pltpu.make_async_copy(a_ref.at[z], t_ref.at[seq, c], loc_sem)

        for step in range(1, blocks):
            outgoing(lax.rem(z + step, blocks)).start()

        @pl.when(seq_core == c)
        def _():
            own().start()

        @pl.when(seq_core != c)
        def _():
            outgoing(z).start()

        for s in range(seqs):
            for k in range(2):
                from_self = (2 * c + s == z) & (c == k)

                @pl.when(jnp.logical_not(from_self))
                def _():
                    remote(a_ref.at[0], t_ref.at[s, k], send_sem.at[0], recv_sem.at[s, k], z, base).wait_recv()

        for step in range(1, blocks):
            outgoing(lax.rem(z + step, blocks)).wait_send()

        @pl.when(seq_core == c)
        def _():
            own().wait()

        @pl.when(seq_core != c)
        def _():
            outgoing(z).wait_send()

    return pl.pallas_call(
        kernel,
        name="attended_exchange",
        out_shape=jax.ShapeDtypeStruct((seqs, 2, span, width), bf16),
        in_specs=[ANY],
        out_specs=ANY,
        scratch_shapes=[DMA, DMA((blocks,)), DMA((seqs, 2))],
        compiler_params=params(2),
    )(att)


def d_attended_exchange(rows, blocks):
    seqs, _, span, width = rows.shape

    def kernel(t_ref, a_ref, loc_sem, send_sem, recv_sem):
        z, e, c, base = place()
        seq_core = z // 2
        greet(column_partners(blocks, z, c, base))

        def outgoing(s, k):
            return remote(
                t_ref.at[s, k], a_ref.at[z], send_sem.at[s, k], recv_sem.at[z], 2 * c + s, base + k
            )

        def own(s, k):
            return pltpu.make_async_copy(t_ref.at[s, k], a_ref.at[z], loc_sem)

        for s in range(seqs):
            for k in range(2):
                to_self = (2 * c + s == z) & (c == k)

                @pl.when(to_self)
                def _():
                    own(s, k).start()

                @pl.when(jnp.logical_not(to_self))
                def _():
                    outgoing(s, k).start()

        for step in range(blocks):
            zs = lax.rem(z + step, blocks)
            if step == 0:

                @pl.when(c == seq_core)
                def _():
                    own(0, 0).wait()

                @pl.when(c != seq_core)
                def _():
                    remote(t_ref.at[0, 0], a_ref.at[z], send_sem.at[0, 0], recv_sem.at[z], z, base).wait_recv()
            else:
                remote(t_ref.at[0, 0], a_ref.at[zs], send_sem.at[0, 0], recv_sem.at[zs], z, base).wait_recv()
        for s in range(seqs):
            for k in range(2):

                @pl.when(jnp.logical_not((2 * c + s == z) & (c == k)))
                def _():
                    outgoing(s, k).wait_send()

    return pl.pallas_call(
        kernel,
        name="d_attended_exchange",
        out_shape=jax.ShapeDtypeStruct((blocks, span, width), bf16),
        in_specs=[ANY],
        out_specs=ANY,
        scratch_shapes=[DMA, DMA((seqs, 2)), DMA((blocks,))],
        compiler_params=params(3),
    )(rows)


def d_normed_exchange(part, blocks):
    _, _, half, width = part.shape
    seqs = 2

    def kernel(p_ref, t_ref, sib_ref, sum_ref, loc_sem, ssend_sem, srecv_sem, send_sem, recv_sem):
        z, e, c, base = place()
        seq_core, seq = z // 2, lax.rem(z, 2)
        greet(column_partners(blocks, z, c, base))

        def to_sibling(j):
            return remote(
                p_ref.at[j, 1 - c], sib_ref.at[j], ssend_sem.at[j], srecv_sem.at[j], z, base + 1 - c
            )

        def outgoing(j):
            return remote(
                sum_ref.at[j], t_ref.at[seq, c], send_sem.at[j], recv_sem.at[seq, c], j, base + seq_core
            )

        def own():
            return pltpu.make_async_copy(sum_ref.at[z], t_ref.at[seq, c], loc_sem)

        order = [lax.rem(z + step, blocks) for step in (2, 3, 1, 0)] if blocks == 4 else [
            lax.rem(z + step + 1, blocks) for step in range(blocks)
        ]
        for j in order:
            to_sibling(j).start()
        for i, j in enumerate(order):
            to_sibling(j).wait_recv()
            sum_ref[j] = (p_ref[j, c].astype(f32) + sib_ref[j].astype(f32)).astype(bf16)
            if i < blocks - 1:
                outgoing(j).start()
            else:

                @pl.when(seq_core == c)
                def _():
                    own().start()

                @pl.when(seq_core != c)
                def _():
                    outgoing(j).start()

        for s in range(seqs):
            for k in range(2):
                from_self = (2 * c + s == z) & (c == k)

                @pl.when(jnp.logical_not(from_self))
                def _():
                    remote(sum_ref.at[0], t_ref.at[s, k], send_sem.at[0], recv_sem.at[s, k], z, base).wait_recv()

        for i, j in enumerate(order):
            to_sibling(j).wait_send()
            if i < blocks - 1:
                outgoing(j).wait_send()

        @pl.when(seq_core == c)
        def _():
            own().wait()

        @pl.when(seq_core != c)
        def _():
            outgoing(z).wait_send()

    return pl.pallas_call(
        kernel,
        name="d_normed_exchange",
        out_shape=jax.ShapeDtypeStruct((seqs, 2, half, width), bf16),
        in_specs=[VMEM],
        out_specs=VMEM,
        scratch_shapes=[
            pltpu.VMEM((blocks, half, width), bf16),
            pltpu.VMEM((blocks, half, width), bf16),
            DMA,
            DMA((blocks,)),
            DMA((blocks,)),
            DMA((blocks,)),
            DMA((seqs, 2)),
        ],
        compiler_params=params(4),
    )(part)


def plane_exchange(arrays, columns, collective_id, name):
    count = len(arrays)

    def kernel(*refs):
        sources, targets = refs[:count], refs[count : 2 * count]
        loc_sem, send_sem, recv_sem = refs[2 * count :]
        z, e, c, base = place()
        col = e // 2
        others = [lax.rem(col + step, columns) for step in range(1, columns)]
        greet([(z, 2 * t + c) for t in others])
        for i in range(count):
            for t in others:
                remote(
                    sources[i].at[t], targets[i].at[col], send_sem.at[i, t], recv_sem.at[i, col], z, 2 * t + c
                ).start()
            pltpu.make_async_copy(sources[i].at[col], targets[i].at[col], loc_sem.at[i]).start()
        for i in range(count):
            pltpu.make_async_copy(sources[i].at[col], targets[i].at[col], loc_sem.at[i]).wait()
            for t in others:
                remote(
                    sources[i].at[t], targets[i].at[t], send_sem.at[i, t], recv_sem.at[i, t], z, 2 * t + c
                ).wait()

    return pl.pallas_call(
        kernel,
        name=name,
        out_shape=[jax.ShapeDtypeStruct(a.shape, a.dtype) for a in arrays],
        in_specs=[ANY] * count,
        out_specs=[ANY] * count,
        scratch_shapes=[DMA((count,)), DMA((count, columns)), DMA((count, columns))],
        compiler_params=params(collective_id),
    )(*arrays)


def attention_forward(length, rows, weights, span):
    total, width = rows.shape
    half = weights.shape[1] // 3
    pairs = half // 128
    blocks = total // span

    def kernel(len_ref, x_ref, w_ref, qkv_ref, att_ref, attt_ref, lse_ref, vt_ref):
        seq_len = len_ref[0]
        for j in range(blocks):
            r = pl.ds(j * span, span)
            qkv_ref[r, :] = dot(x_ref[r, :], w_ref[...]).astype(bf16)
        lane = lax.broadcasted_iota(jnp.int32, (1, 128), 1)
        key_place = lax.broadcasted_iota(jnp.int32, (total, 1), 0)
        key_bias = jnp.where(key_place < seq_len, 0.0, masked_fill)
        later = lax.broadcasted_iota(jnp.int32, (span, span), 0) > lax.broadcasted_iota(
            jnp.int32, (span, span), 1
        )

        def pair_step(p, _):
            first = pl.multiple_of(p * 128, 128)
            k_all = qkv_ref[:, pl.ds(half + first, 128)]
            vt_ref[...] = jnp.transpose(qkv_ref[:, pl.ds(2 * half + first, 128)])
            k_heads = []
            for h in range(2):
                inside = (lane // HEAD) == h
                spare = lane == (1 - h) * HEAD
                k_heads.append(
                    jnp.where(
                        inside, k_all.astype(f32), jnp.where(spare, key_bias, 0.0)
                    ).astype(bf16)
                )
            for j in range(blocks):
                n = (j + 1) * span
                r = pl.ds(j * span, span)
                q = qkv_ref[r, pl.ds(first, 128)].astype(f32) * (HEAD**-0.5)
                out_t = []
                for h in range(2):
                    inside = (lane // HEAD) == h
                    spare = lane == (1 - h) * HEAD
                    q_h = jnp.where(inside, q, jnp.where(spare, 1.0, 0.0)).astype(bf16)
                    s = dot_nt(k_heads[h][:n], q_h)
                    last = jnp.where(later, masked_fill, s[n - span :])
                    s = last if j == 0 else jnp.concatenate([s[: n - span], last], axis=0)
                    top = jnp.max(s, axis=0, keepdims=True)
                    w = jnp.exp(s - top)
                    total_w = jnp.sum(w, axis=0, keepdims=True)
                    o_t = dot(vt_ref[h * HEAD : (h + 1) * HEAD, :n], w.astype(bf16))
                    out_t.append(o_t / total_w)
                    lse_ref[pl.ds(2 * p + h, 1), r] = top + jnp.log(total_w)
                o = jnp.concatenate(out_t, axis=0)
                attt_ref[pl.ds(first, 128), r] = o
                att_ref[j, :, pl.ds(first, 128)] = jnp.transpose(o).astype(bf16)
            return 0

        lax.fori_loop(0, pairs, pair_step, 0)

    return pl.pallas_call(
        kernel,
        name="attention_forward",
        out_shape=[
            jax.ShapeDtypeStruct((total, 3 * half), bf16),
            jax.ShapeDtypeStruct((blocks, span, half), bf16),
            jax.ShapeDtypeStruct((half, total), f32),
            jax.ShapeDtypeStruct((2 * pairs, total), f32),
        ],
        in_specs=[SMEM, VMEM, VMEM],
        out_specs=[VMEM] * 4,
        scratch_shapes=[pltpu.VMEM((128, total), bf16)],
        compiler_params=pltpu.CompilerParams(vmem_limit_bytes=VMEM_BYTES),
        cost_estimate=pl.CostEstimate(flops=20 * 10**9, bytes_accessed=10**7, transcendentals=0),
    )(length, rows, weights)


def attention_backward(length, rows, weights, qkv, att_t, lse, d_att, span):
    total, width = rows.shape
    half = weights.shape[1] // 3
    pairs = half // 128
    blocks = total // span
    scale = HEAD**-0.5

    def kernel(
        len_ref, x_ref, w_ref, qkv_ref, attt_ref, lse_ref, do_ref, gw_ref, dn_ref, dqkv_ref, kt_ref, dk_ref, dv_ref
    ):
        seq_len = len_ref[0]
        lane = lax.broadcasted_iota(jnp.int32, (1, 128), 1)
        key_place = lax.broadcasted_iota(jnp.int32, (total, 1), 0)
        key_bias = jnp.where(key_place < seq_len, 0.0, masked_fill)
        later = lax.broadcasted_iota(jnp.int32, (span, span), 0) > lax.broadcasted_iota(
            jnp.int32, (span, span), 1
        )

        def pair_step(p, _):
            first = pl.multiple_of(p * 128, 128)
            k_all = qkv_ref[:, pl.ds(half + first, 128)]
            kt_ref[...] = jnp.transpose(k_all)
            v_all = qkv_ref[:, pl.ds(2 * half + first, 128)]
            k_heads = []
            for h in range(2):
                inside = (lane // HEAD) == h
                spare = lane == (1 - h) * HEAD
                k_heads.append(
                    jnp.where(
                        inside, k_all.astype(f32), jnp.where(spare, key_bias, 0.0)
                    ).astype(bf16)
                )
            dk_ref[...] = jnp.zeros_like(dk_ref)
            dv_ref[...] = jnp.zeros_like(dv_ref)
            for j in range(blocks):
                n = (j + 1) * span
                r = pl.ds(j * span, span)
                q = qkv_ref[r, pl.ds(first, 128)].astype(f32) * scale
                d_o = do_ref[r, pl.ds(first, 128)].astype(f32)
                prod_t = jnp.transpose(d_o) * attt_ref[pl.ds(first, 128), r]
                dq_t = []
                for h in range(2):
                    inside = (lane // HEAD) == h
                    spare = lane == (1 - h) * HEAD
                    q_h = jnp.where(inside, q, jnp.where(spare, 1.0, 0.0)).astype(bf16)
                    q_only = jnp.where(inside, q, 0.0).astype(bf16)
                    do_h = jnp.where(inside, d_o, 0.0).astype(bf16)
                    delta = jnp.sum(prod_t[h * HEAD : (h + 1) * HEAD], axis=0, keepdims=True)
                    s = dot_nt(k_heads[h][:n], q_h)
                    last = jnp.where(later, masked_fill, s[n - span :])
                    s = last if j == 0 else jnp.concatenate([s[: n - span], last], axis=0)
                    w = jnp.exp(s - lse_ref[pl.ds(2 * p + h, 1), r])
                    d_w = dot_nt(v_all[:n], do_h)
                    d_s = (w * (d_w - delta)).astype(bf16)
                    dv_ref[:n] += dot(w.astype(bf16), do_h)
                    dk_ref[:n] += dot(d_s, q_only)
                    dq_t.append(dot(kt_ref[h * HEAD : (h + 1) * HEAD, :n], d_s))
                dq = jnp.transpose(jnp.concatenate(dq_t, axis=0)) * scale
                dqkv_ref[r, pl.ds(first, 128)] = dq.astype(bf16)
            dqkv_ref[:, pl.ds(half + first, 128)] = dk_ref[...].astype(bf16)
            dqkv_ref[:, pl.ds(2 * half + first, 128)] = dv_ref[...].astype(bf16)
            return 0

        lax.fori_loop(0, pairs, pair_step, 0)
        for j in range(blocks):
            r = pl.ds(j * span, span)
            dn_ref[j] = dot_nt(dqkv_ref[r, :], w_ref[...]).astype(bf16)
        for m in range(3):
            gw_ref[m] = dot_tn(x_ref[...], dqkv_ref[:, m * half : (m + 1) * half]).astype(bf16)

    return pl.pallas_call(
        kernel,
        name="attention_backward",
        out_shape=[
            jax.ShapeDtypeStruct((3, width, half), bf16),
            jax.ShapeDtypeStruct((blocks, span, width), bf16),
        ],
        in_specs=[SMEM] + [VMEM] * 6,
        out_specs=[VMEM] * 2,
        scratch_shapes=[
            pltpu.VMEM((total, 3 * half), bf16),
            pltpu.VMEM((128, total), bf16),
            pltpu.VMEM((total, 128), f32),
            pltpu.VMEM((total, 128), f32),
        ],
        compiler_params=pltpu.CompilerParams(vmem_limit_bytes=VMEM_BYTES),
        cost_estimate=pl.CostEstimate(flops=40 * 10**9, bytes_accessed=10**7, transcendentals=0),
    )(length, rows, weights, qkv, att_t, lse, d_att)


def experts(rows, d_out, inner_own, inner_sib, outer_own, outer_sib):
    total, width = rows.shape
    steps, _, part = inner_own.shape
    block = 256

    def kernel(
        x_ref, d_ref, io_ref, is_ref, oo_ref, os_ref,
        out_ref, dx_ref, gio_ref, gis_ref, goo_ref, gos_ref,
        oacc_ref, dacc_ref, act_ref, dpre_ref, wi_ref, wo_ref,
    ):
        g = pl.program_id(0)
        wi_ref[:, :part] = io_ref[0]
        wi_ref[:, part:] = is_ref[0]
        wo_ref[:part] = oo_ref[0]
        wo_ref[part:] = os_ref[0]

        @pl.when(g == 0)
        def _():
            oacc_ref[...] = jnp.zeros_like(oacc_ref)
            dacc_ref[...] = jnp.zeros_like(dacc_ref)

        def row_step(b, _):
            r = pl.ds(pl.multiple_of(b * block, block), block)
            pre = dot(x_ref[r, :], wi_ref[...])
            cdf = 0.5 * (1.0 + lax.erf(pre * (0.5**0.5)))
            act = (pre * cdf).astype(bf16)
            slope = cdf + pre * (jnp.exp(-0.5 * pre * pre) * ((2 * jnp.pi) ** -0.5))
            d_act = dot_nt(d_ref[r, :], wo_ref[...])
            d_pre = (d_act * slope).astype(bf16)
            act_ref[r, :] = act
            dpre_ref[r, :] = d_pre
            oacc_ref[r, :] += dot(act, wo_ref[...])
            dacc_ref[r, :] += dot_nt(d_pre, wi_ref[...])
            return 0

        lax.fori_loop(0, total // block, row_step, 0)
        g_inner = dot_tn(x_ref[...], dpre_ref[...]).astype(bf16)
        gio_ref[0] = g_inner[:, :part]
        gis_ref[0] = g_inner[:, part:]
        g_outer = dot_tn(act_ref[...], d_ref[...]).astype(bf16)
        goo_ref[0] = g_outer[:part]
        gos_ref[0] = g_outer[part:]

        @pl.when(g == steps - 1)
        def _():
            out_ref[...] = oacc_ref[...].astype(bf16)
            dx_ref[...] = dacc_ref[...].astype(bf16)

    whole = pl.BlockSpec((total, width), lambda g: (0, 0))
    inner = pl.BlockSpec((1, width, part), lambda g: (g, 0, 0))
    outer = pl.BlockSpec((1, part, width), lambda g: (g, 0, 0))
    return pl.pallas_call(
        kernel,
        name="experts",
        grid=(steps,),
        out_shape=[
            jax.ShapeDtypeStruct((total, width), bf16),
            jax.ShapeDtypeStruct((total, width), bf16),
            jax.ShapeDtypeStruct((steps, width, part), bf16),
            jax.ShapeDtypeStruct((steps, width, part), bf16),
            jax.ShapeDtypeStruct((steps, part, width), bf16),
            jax.ShapeDtypeStruct((steps, part, width), bf16),
        ],
        in_specs=[whole, whole, inner, inner, outer, outer],
        out_specs=[whole, whole, inner, inner, outer, outer],
        scratch_shapes=[
            pltpu.VMEM((total, width), f32),
            pltpu.VMEM((total, width), f32),
            pltpu.VMEM((total, 2 * part), bf16),
            pltpu.VMEM((total, 2 * part), bf16),
            pltpu.VMEM((width, 2 * part), bf16),
            pltpu.VMEM((2 * part, width), bf16),
        ],
        compiler_params=pltpu.CompilerParams(
            vmem_limit_bytes=VMEM_BYTES, dimension_semantics=("arbitrary",)
        ),
        cost_estimate=pl.CostEstimate(flops=40 * 10**9, bytes_accessed=3 * 10**7, transcendentals=0),
    )(rows, d_out, inner_own, inner_sib, outer_own, outer_sib)


def expert_grad_sum(gi_own, gi_sib, go_own, go_sib):
    blocks, width, part = gi_own.shape

    def kernel(
        gio_ref, gis_ref, goo_ref, gos_ref, fi_ref, fo_ref,
        oi, oo, si, so, zi, zo, loc_sem, ssend_sem, srecv_sem, send_sem, recv_sem,
    ):
        z, e, c, base = place()
        greet(column_partners(blocks, z, c, base))
        order = [lax.rem(z + step, blocks) for step in (2, 1, 3, 0)] if blocks == 4 else [
            lax.rem(z + step + 1, blocks) for step in range(blocks)
        ]

        def sibling(i, src, dst, j):
            return remote(src.at[j], dst.at[j], ssend_sem.at[i, j], srecv_sem.at[i, j], z, base + 1 - c)

        def local(i, src, dst, j):
            return pltpu.make_async_copy(src.at[j], dst.at[j], loc_sem.at[i, j])

        def over_z(i, src, dst, j):
            return remote(src.at[j], dst.at[z], send_sem.at[i, j], recv_sem.at[i, z], j, e)

        for j in order:
            sibling(0, gis_ref, si, j).start()
            sibling(1, gos_ref, so, j).start()
            local(0, gio_ref, oi, j).start()
            local(1, goo_ref, oo, j).start()
        for n, j in enumerate(order):
            for i, (own, sib, src, ssrc) in enumerate(((oi, si, gio_ref, gis_ref), (oo, so, goo_ref, gos_ref))):
                local(i, src, own, j).wait()
                sibling(i, ssrc, sib, j).wait_recv()
                own[j] = (own[j].astype(f32) + sib[j].astype(f32)).astype(bf16)
                if n < blocks - 1:
                    over_z(i, own, (zi, zo)[i], j).start()
        for i, (own, into, out) in enumerate(((oi, zi, fi_ref), (oo, zo, fo_ref))):
            for step in range(1, blocks):
                zs = lax.rem(z + step, blocks)
                remote(own.at[0], into.at[zs], send_sem.at[i, 0], recv_sem.at[i, zs], z, e).wait_recv()
            into[z] = own[z]
            acc = into[0].astype(f32)
            for j in range(1, blocks):
                acc = acc + into[j].astype(f32)
            out[...] = acc
        for n, j in enumerate(order):
            for i, (own, ssrc, sib) in enumerate(((oi, gis_ref, si), (oo, gos_ref, so))):
                sibling(i, ssrc, sib, j).wait_send()
                if n < blocks - 1:
                    over_z(i, own, (zi, zo)[i], j).wait_send()

    return pl.pallas_call(
        kernel,
        name="expert_grad_sum",
        out_shape=[
            jax.ShapeDtypeStruct((width, part), f32),
            jax.ShapeDtypeStruct((part, width), f32),
        ],
        in_specs=[ANY] * 4,
        out_specs=[VMEM] * 2,
        scratch_shapes=[
            pltpu.VMEM((blocks, width, part), bf16),
            pltpu.VMEM((blocks, part, width), bf16),
            pltpu.VMEM((blocks, width, part), bf16),
            pltpu.VMEM((blocks, part, width), bf16),
            pltpu.VMEM((blocks, width, part), bf16),
            pltpu.VMEM((blocks, part, width), bf16),
            DMA((2, blocks)),
            DMA((2, blocks)),
            DMA((2, blocks)),
            DMA((2, blocks)),
            DMA((2, blocks)),
        ],
        compiler_params=params(5),
    )(gi_own, gi_sib, go_own, go_sib)


def dense_grad_sum(qkv_part, out_part, small, blocks, columns):
    _, width, half = qkv_part.shape
    bits = max(1, columns.bit_length() - 1)
    assert columns == 1 << bits and bits >= 2
    piece = 4 * width // (8 * blocks)
    rest = bits - 2

    def kernel(
        q_ref, o_ref, s_ref, g_ref, t_ref,
        work, got1, got2, got3, gotr, osib, sgot, szgot, sem, rsem, zsem, zrsem, ssem, srsem,
    ):
        z, e, c, base = place()
        col = e // 2
        sib = base + 1 - c
        bit = [lax.rem(col // (1 << i), 2) for i in range(bits)]
        mate = [2 * (col + (1 - 2 * bit[i]) * (1 << i)) + c for i in range(bits)]
        greet(
            [(z, sib)]
            + [(z, mate[i]) for i in range(bits)]
            + [(lax.rem(z + step, blocks), e) for step in range(1, blocks)]
        )
        count = [0]

        def swap(src, dst, target_z, target_e):
            i = count[0]
            count[0] += 1
            copy = remote(src, dst, sem.at[i], rsem.at[i], target_z, target_e)
            copy.start()
            return copy

        def add(into, index, received):
            into[index] = (into[index].astype(f32) + received.astype(f32)).astype(bf16)

        scount = [0]

        def small_swap(target_z, target_e):
            i = scount[0]
            scount[0] += 1
            copy = remote(t_ref, sgot.at[i], ssem.at[i], srsem.at[i], target_z, target_e)
            copy.start()
            return copy, i

        def small_add(copy, i):
            copy.wait()
            t_ref[...] = t_ref[...] + sgot[i]

        t_ref[...] = s_ref[...]
        first = swap(o_ref.at[1 - c], osib, z, sib)
        tiny, n = small_swap(z, sib)
        rows = 2 * 2 * blocks * piece
        work[0] = jnp.concatenate([q_ref[0], q_ref[1]], axis=0).reshape(2, 2, blocks, piece, half)
        first.wait()
        o_sum = (o_ref[c].astype(f32) + osib[...].astype(f32)).astype(bf16)
        work[1] = jnp.concatenate([q_ref[2], o_sum], axis=0).reshape(2, 2, blocks, piece, half)
        small_add(tiny, n)
        one = [swap(work.at[i, 1 - bit[i]], got1.at[i], z, mate[i]) for i in range(2)]
        tiny, n = small_swap(z, mate[0])
        for i in range(2):
            one[i].wait()
            work[i, bit[i]] = (work[i, bit[i]].astype(f32) + got1[i].astype(f32)).astype(bf16)
        small_add(tiny, n)
        two = [swap(work.at[i, bit[i], 1 - bit[1 - i]], got2.at[i], z, mate[1 - i]) for i in range(2)]
        tiny, n = small_swap(z, mate[1])
        for i in range(2):
            two[i].wait()
            work[i, bit[i], bit[1 - i]] = (
                work[i, bit[i], bit[1 - i]].astype(f32) + got2[i].astype(f32)
            ).astype(bf16)
        small_add(tiny, n)
        sends = []
        for step in range(1, blocks):
            zt = lax.rem(z + step, blocks)
            for i in range(2):
                copy = remote(
                    work.at[i, bit[i], bit[1 - i], zt], got3.at[i, z], zsem.at[i, zt], zrsem.at[i, z], zt, e
                )
                copy.start()
                sends.append(copy)
            copy = remote(t_ref, szgot.at[z], zsem.at[2, zt], zrsem.at[4, z], zt, e)
            copy.start()
            sends.append(copy)
        for step in range(1, blocks):
            zs = lax.rem(z + step, blocks)
            for i in range(2):
                remote(got3.at[i, 0], got3.at[i, zs], zsem.at[i, zs], zrsem.at[i, zs], z, e).wait_recv()
            remote(t_ref, szgot.at[zs], zsem.at[2, zs], zrsem.at[4, zs], z, e).wait_recv()
        for copy in sends:
            copy.wait_send()
        szgot[z] = t_ref[...]
        tot = szgot[0]
        for j in range(1, blocks):
            tot = tot + szgot[j]
        t_ref[...] = tot
        for i in range(2):
            got3[i, z] = work[i, bit[i], bit[1 - i], z]
            tot = got3[i, 0].astype(f32)
            for j in range(1, blocks):
                tot = tot + got3[i, j].astype(f32)
            g_ref[c, i, bit[i], bit[1 - i], z] = tot.astype(bf16)
        for b in range(rest):
            got = [
                swap(g_ref.at[c, i, bit[i], bit[1 - i], z], gotr.at[b, i], z, mate[2 + b]) for i in range(2)
            ]
            tiny, n = small_swap(z, mate[2 + b])
            for i in range(2):
                got[i].wait()
                g_ref[c, i, bit[i], bit[1 - i], z] = (
                    g_ref[c, i, bit[i], bit[1 - i], z].astype(f32) + gotr[b, i].astype(f32)
                ).astype(bf16)
            small_add(tiny, n)
        sends = []
        for step in range(1, blocks):
            zt = lax.rem(z + step, blocks)
            for i in range(2):
                at = g_ref.at[c, i, bit[i], bit[1 - i], z]
                copy = remote(at, at, zsem.at[i, zt], zrsem.at[2 + i, z], zt, e)
                copy.start()
                sends.append(copy)
        for step in range(1, blocks):
            zs = lax.rem(z + step, blocks)
            for i in range(2):
                at = g_ref.at[c, i, bit[i], bit[1 - i], zs]
                remote(at, at, zsem.at[i, zs], zrsem.at[2 + i, zs], z, e).wait_recv()
        for copy in sends:
            copy.wait_send()
        two = []
        for i in range(2):
            at = g_ref.at[c, i, bit[i], bit[1 - i]]
            two.append(swap(at, at, z, mate[1 - i]))
        for copy in two:
            copy.wait()
        one = []
        for i in range(2):
            at = g_ref.at[c, i, bit[i]]
            one.append(swap(at, at, z, mate[i]))
        for copy in one:
            copy.wait()
        swap(g_ref.at[c], g_ref.at[c], z, sib).wait()

    lanes = small.shape
    stages = 2 + 2 + 2 + 2 * rest + 2 + 2 + 2
    work_shape = (2, 2, 2, blocks, piece, half)
    grads, sums = pl.pallas_call(
        kernel,
        name="dense_grad_sum",
        out_shape=[
            jax.ShapeDtypeStruct((2,) + work_shape, bf16),
            jax.ShapeDtypeStruct(lanes, f32),
        ],
        in_specs=[VMEM] * 3,
        out_specs=[VMEM] * 2,
        scratch_shapes=[
            pltpu.VMEM(work_shape, bf16),
            pltpu.VMEM((2, 2, blocks, piece, half), bf16),
            pltpu.VMEM((2, blocks, piece, half), bf16),
            pltpu.VMEM((2, blocks, piece, half), bf16),
            pltpu.VMEM((max(1, rest), 2, piece, half), bf16),
            pltpu.VMEM((width, half), bf16),
            pltpu.VMEM((1 + bits,) + lanes, f32),
            pltpu.VMEM((blocks,) + lanes, f32),
            DMA((stages,)),
            DMA((stages,)),
            DMA((3, blocks)),
            DMA((5, blocks)),
            DMA((1 + bits,)),
            DMA((1 + bits,)),
        ],
        compiler_params=params(6),
    )(qkv_part, out_part, small)
    return grads.reshape(2, 4, width, half), sums


def layer_norm(inputs, norm_gain, norm_shift):
    centered = inputs - jnp.mean(inputs, axis=-1, keepdims=True)
    variance = jnp.mean(centered * centered, axis=-1, keepdims=True)
    return centered * lax.rsqrt(variance + epsilon) * norm_gain + norm_shift


def on_device(
    hidden_in,
    cotangent,
    query_weight,
    key_weight,
    value_weight,
    output_weight,
    gain_one,
    shift_one,
    gain_two,
    shift_two,
    w_router,
    w_inner,
    w_outer,
    expert_ids,
    seq_lengths,
):
    seqs, span, width = hidden_in.shape
    tokens = seqs * span
    blocks = lax.axis_size("blk")
    columns = lax.axis_size("ep") // 2
    experts_n = w_router.shape[1]
    capacity = max(2, 2 * tokens // experts_n)
    slots = experts_n * capacity
    half = width // 2
    assert seqs * 2 == blocks and experts_n == columns
    z, e, c, base = place()

    inner_own = lax.all_gather(w_inner[0], "blk", axis=0)
    outer_own = lax.all_gather(w_outer[0], "blk", axis=0)
    flip = [(i, i ^ 1) for i in range(2 * columns)]
    inner_sib = lax.ppermute(inner_own, "ep", flip)
    outer_sib = lax.ppermute(outer_own, "ep", flip)

    inputs = hidden_in.astype(f32)
    normed_f, norm_one_pull = jax.vjp(layer_norm, inputs, gain_one, shift_one)
    normed = normed_f.astype(bf16)

    token_experts = expert_ids.reshape(tokens)
    onehot = token_experts[:, None] == jnp.arange(experts_n, dtype=jnp.int32)[None, :]
    onehot_f = onehot.astype(f32)
    onehot_int = onehot.astype(jnp.int32)
    places = z * span + jnp.arange(span, dtype=jnp.int32)
    valid_rows = (places[None, :] < seq_lengths[:, None]).astype(f32).reshape(tokens)
    counts = lax.psum(jnp.sum(onehot_f * valid_rows[:, None], axis=0), ("blk", "ep"))
    mean_load = jnp.sum(counts) / experts_n
    load_ratio = (counts - mean_load) / mean_load
    slot_ranks = jnp.sum(jnp.cumsum(onehot_int, axis=0) * onehot_int, axis=1) - 1
    slot_rows = token_experts * capacity + slot_ranks
    to_slots = (jnp.arange(slots, dtype=jnp.int32)[:, None] == slot_rows[None, :]).astype(bf16)
    from_slots = (slot_rows[:, None] == jnp.arange(slots, dtype=jnp.int32)[None, :]).astype(bf16)

    column_lengths = lax.all_gather(seq_lengths, "ep")
    length = lax.dynamic_slice(
        column_lengths, (base + z // 2, lax.rem(z, 2)), (1, 1)
    ).reshape(1)

    def half_columns(weight):
        return lax.dynamic_slice_in_dim(weight, c * half, half, axis=1)

    w_qkv = jnp.concatenate(
        [half_columns(query_weight), half_columns(key_weight), half_columns(value_weight)], axis=1
    )

    rows_all = normed_exchange(normed, blocks)
    qkv, att, att_t, lse = attention_forward(length, rows_all, w_qkv, span)
    attended = attended_exchange(att, blocks)

    branch = jnp.einsum(
        "skqd,kde->sqe", attended, output_weight.reshape(2, half, width), preferred_element_type=f32
    )
    middle = (inputs + branch).reshape(tokens, width)
    normed_two_f, norm_two_pull = jax.vjp(layer_norm, middle, gain_two, shift_two)
    flat_rows = normed_two_f.astype(bf16)
    logits = jnp.dot(flat_rows, w_router, preferred_element_type=f32)
    gate_values = jax.nn.sigmoid(jnp.sum(logits * onehot_f, axis=1))
    scale_rows = valid_rows * gate_values
    grad_flat = cotangent.astype(f32).reshape(tokens, width)
    d_expert = (scale_rows[:, None] * grad_flat).astype(bf16)

    sent = jnp.dot(to_slots, jnp.concatenate([flat_rows, d_expert], axis=1), preferred_element_type=f32).astype(bf16)
    to_rows = sent[:, :width].reshape(columns, capacity, width)
    to_grads = sent[:, width:].reshape(columns, capacity, width)
    got_rows, got_grads = plane_exchange([to_rows, to_grads], columns, 7, "dispatch_exchange")
    produced, d_rows, gi_own, gi_sib, go_own, go_sib = experts(
        got_rows.reshape(-1, width),
        got_grads.reshape(-1, width),
        inner_own,
        inner_sib,
        outer_own,
        outer_sib,
    )
    back_rows, back_grads = plane_exchange(
        [
            produced.reshape(columns, capacity, width),
            d_rows.reshape(columns, capacity, width),
        ],
        columns,
        8,
        "return_exchange",
    )
    expert_out = jnp.dot(from_slots, back_rows.reshape(slots, width), preferred_element_type=f32)
    d_expert_rows = jnp.dot(from_slots, back_grads.reshape(slots, width), preferred_element_type=f32)

    output = (middle + scale_rows[:, None] * expert_out).reshape(seqs, span, width).astype(bf16)
    ratio_rows = jnp.sum(onehot_f * load_ratio[None, :], axis=1)
    local_balance = jnp.sum(scale_rows * ratio_rows)
    d_gate = valid_rows * (jnp.sum(grad_flat * expert_out, axis=1) + balance_weight * ratio_rows)
    d_logits = (onehot_f * (d_gate * gate_values * (1.0 - gate_values))[:, None]).astype(bf16)
    grad_router = jnp.einsum("td,te->ed", flat_rows, d_logits, preferred_element_type=f32)
    d_router_rows = jnp.einsum("te,de->td", d_logits, w_router, preferred_element_type=f32)
    d_middle_norm, grad_gain_two, grad_shift_two = norm_two_pull(d_expert_rows + d_router_rows)
    d_middle = (grad_flat + d_middle_norm).reshape(seqs, span, width)
    d_branch = d_middle.astype(bf16)
    out_part = jnp.einsum(
        "skqd,sqhe->hkde", attended, d_branch.reshape(seqs, span, 2, half), preferred_element_type=f32
    ).astype(bf16).reshape(2, width, half)
    d_attended = jnp.einsum(
        "sqe,kde->skqd", d_branch, output_weight.reshape(2, half, width), preferred_element_type=f32
    ).astype(bf16)
    d_att = d_attended_exchange(d_attended, blocks)
    qkv_part, d_norm_part = attention_backward(
        length, rows_all, w_qkv, qkv, att_t, lse, d_att.reshape(blocks * span, half), span
    )
    d_normed = d_normed_exchange(d_norm_part.reshape(blocks, 2, span // 2, width), blocks)
    d_input_norm, grad_gain_one, grad_shift_one = norm_one_pull(
        d_normed.reshape(seqs, span, width).astype(f32)
    )
    grad_hidden = d_middle + d_input_norm

    vectors = jnp.concatenate(
        [
            grad_gain_one[None],
            grad_shift_one[None],
            grad_gain_two[None],
            grad_shift_two[None],
            grad_router,
            jnp.full((1, width), local_balance, f32),
        ],
        axis=0,
    )
    pad = -vectors.shape[0] % 8
    vectors = jnp.pad(vectors, ((0, pad), (0, 0)))
    grads, sums = dense_grad_sum(qkv_part, out_part, vectors, blocks, columns)
    dense = [
        jnp.concatenate([grads[0, m], grads[1, m]], axis=1).astype(f32) for m in range(4)
    ]
    grad_inner, grad_outer = expert_grad_sum(gi_own, gi_sib, go_own, go_sib)
    balance = sums[4 + experts_n, 0] / jnp.sum(counts)
    return (
        output,
        grad_hidden,
        dense[0],
        dense[1],
        dense[2],
        dense[3],
        sums[0],
        sums[1],
        sums[2],
        sums[3],
        jnp.transpose(sums[4 : 4 + experts_n]),
        grad_inner[None],
        grad_outer[None],
        balance,
    )


def solution(mesh):
    tokens = P("ep", "blk", None)
    return jax.shard_map(
        on_device,
        mesh=mesh,
        in_specs=(tokens, tokens)
        + (P(),) * 9
        + (P("ep", None, "blk"), P("ep", "blk", None), P("ep", "blk", None, None, None), P("ep")),
        out_specs=(tokens, tokens) + (P(),) * 9 + (P("ep", None, "blk"), P("ep", "blk", None), P()),
        check_vma=False,
    )
```

time: 1670 us -> 630 us (0.38)
  waiting for transfers between devices: 1120 us -> 1.38 us
  Pallas kernels: 0 us -> 486 us
  matrix products: 185 us -> 10.8 us
  blocking collectives: 211 us -> 45 us
  local copies, waits for them, and re-layouts: 64.6 us -> 28.2 us
  other arithmetic: 48.9 us -> 32 us
    reduce_scatter x3 -> x0, waiting for transfers between devices: 560 us -> none  [the longest x1 210 us: on_device(): lax.psum_scatter(jnp.dot(act_part, outer_weight, preferred_element_type=f...]
    pallas_call x0 -> x11, Pallas kernels: none -> 486 us  [the longest x1 109 us: expert_grad_sum(): pl.pallas_call(kernel, name='expert_grad_sum', out_shape=[jax.ShapeDtypeS...]
    all_gather x4 -> x2, waiting for transfers between devices: 415 us -> 0.01 us  [the longest x1 0.01 us: on_device(): inner_own = lax.all_gather(w_inner[0], 'blk', axis=0)]
    dot_general x33 -> x7, matrix products: 182 us -> 9.35 us  [the longest x1 1.99 us: on_device(): jnp.einsum('skqd,kde->sqe', attended, output_weight.reshape(2, half, widt...]
    psum x1 -> x0, waiting for transfers between devices: 112 us -> none  [on_device(): lax.psum((grad_query, grad_key, grad_value, grad_out, grad_gain_one, grad...]
    all_to_all x2 -> x0, blocking collectives: 82 us -> none  [the longest x1 41 us: on_device(): lax.all_to_all(both_halves(d_send), 'ep', split_axis=0, concat_axis=0, ti...]
    psum x1, blocking collectives: 87.7 us -> 38.5 us  [on_device(): lax.psum(jnp.sum(onehot_f * valid_rows[:, None], axis=0), ('blk', 'ep'))]
    psum x1 -> x0, blocking collectives: 41.1 us -> none  [on_device(): lax.psum((grad_query, grad_key, grad_value, grad_out, grad_gain_one, grad...]
  transfers between devices with their start and end apart: 10 -> 4, of which waited for: 9 -> 0; matrix products, arithmetic and copies ran while one was open for 7% -> 5% of each run, Pallas kernels for 0% -> 24%
where the time goes in v1:
time: 630 us; the launch traced here: 623 us
  Pallas kernels  486 us (77%)
  blocking collectives  45 us (7%)
  other arithmetic  32 us (5%)
  local copies, waits for them, and re-layouts  28.2 us (4%)
  between operations  18.8 us (3%)
  matrix products  10.8 us (2%)
    pallas_call x1, Pallas kernels, expert_grad_sum(): pl.pallas_call(kernel, name='expert_grad_sum', out_shape=[jax.ShapeDtypeS...  109 us
    pallas_call x1, Pallas kernels, dense_grad_sum(): pl.pallas_call(kernel, name='dense_grad_sum', out_shape=[jax.ShapeDtypeSt...  87 us
    pallas_call x2, Pallas kernels, plane_exchange(): pl.pallas_call(kernel, name=name, out_shape=[jax.ShapeDtypeStruct(a.shape...  73.6 us
    pallas_call x1, Pallas kernels, normed_exchange(): pl.pallas_call(kernel, name='normed_exchange', out_shape=jax.ShapeDtypeSt...  58.9 us
    pallas_call x1, Pallas kernels, experts(): pl.pallas_call(kernel, name='experts', grid=(steps,), out_shape=[jax.Shap...  38.9 us
    psum x1, blocking collectives, on_device(): lax.psum(jnp.sum(onehot_f * valid_rows[:, None], axis=0), ('blk', 'ep'))  38.5 us
    pallas_call x1, Pallas kernels, attended_exchange(): pl.pallas_call(kernel, name='attended_exchange', out_shape=jax.ShapeDtype...  38.4 us
    pallas_call x1, Pallas kernels, d_attended_exchange(): pl.pallas_call(kernel, name='d_attended_exchange', out_shape=jax.ShapeDty...  22.3 us
  transfers between devices with their start and end apart: 4, of which 0 were waited for; matrix products, arithmetic and copies ran while one was open for 5% of the time, Pallas kernels for 24%

profile of v1, /device:TPU:9, one launch (start us, length us, event | category | flops | bytes accessed | tf_op | source)
XLA Modules:
  0.0 622.5 jit_solution(12100563244858768804)
XLA Ops:
  8.7 1.2 dynamic-slice
  10.6 0.9 dynamic-update-slice
  11.6 6.5 %all-reduce.2 = s32[8,2]{1,0:T(8,128)S(1)} all-reduce(s32[8,2]{1,0:T(8,128)S(1)} %reshape.312), channel_id=2, replica_groups=mesh['blk'=4,'ep'=8] {'ep'}, use_global_device_ids=true, to_apply=%add.1 | all-reduce | flops 16 | bytes 128
  19.2 58.9 %normed_exchange.1 = bf16[4,2,128,768]{3,2,1,0:T(8,128)(2,1)S(1)} custom-call(bf16[2,2,128,768]{3,2,1,0:T(8,128)(2,1)S(1)} %bitcast.130), custom_call_target="tpu_custom_call" | custom-call | tf_op jit(solution)/shard_map/normed_exchange/pallas_call | solution.py:132
  78.2 2.0 constant_dynamic-slice_fusion.2
  80.2 2.0 constant_dynamic-slice_fusion
  82.2 2.7 pad_maximum_fusion.w_ref
  85.5 16.3 %attention_forward.1 = (bf16[1024,1152]{1,0:T(8,128)(2,1)}, bf16[4,256,384]{2,1,0:T(8,128)(2,1)S(1)}, f32[384,1024]{1,0:T(8,128)S(1)}, f32[6,1024]{1,0:T(8,128)S(1)}) custom-call(s32[1]{0:T(128)} %bitcast.1.len_ref, bf16[1024,768]{1,0:T(8,128)(2,1)S(1)} %bitcast.131, bf16[768,1152]{1,0:T(8,128)(2,1)} %pad_maximum_fusion.w_ref), custom_call_target="tpu_custom_call" | custom-call | flops 20000000000 | bytes 10000000 | tf_op jit(solution)/shard_map/attention_forward/pallas_call | solution.py:432
  101.8 1.1 copy-done.7
  103.6 38.4 %attended_exchange.1 = bf16[2,2,256,384]{3,2,1,0:T(8,128)(2,1)S(1)} custom-call(bf16[4,256,384]{2,1,0:T(8,128)(2,1)S(1)} %get-tuple-element.34.a_ref), custom_call_target="tpu_custom_call" | custom-call | tf_op jit(solution)/shard_map/attended_exchange/pallas_call | solution.py:190
  143.3 2.3 reduce-window.6
  146.4 1.4 reduce-window.9
  147.8 1.3 select_reduce_fusion.1
  149.1 2.0 fusion.48
  152.3 0.9 multiply_reduce_fusion.2
  155.0 38.5 %psum.7 = f32[4]{0:T(128)} all-reduce(f32[4]{0:T(128)} %select_reduce_fusion.1), channel_id=1, replica_groups=mesh['blk'=4,'ep'=8] {'blk','ep'}, use_global_device_ids=true, to_apply=%region_10.11 | all-reduce | flops 4 | bytes 32 | tf_op jit(solution)/shard_map/psum | solution.py:916
  194.8 1.3 reduce_sum.181
  198.2 1.8 add_convert_fusion
  200.1 1.0 fusion.22
  201.9 1.8 convolution_convert_fusion
  203.7 1.9 fusion.47
  205.6 37.9 %dispatch_exchange.1 = (bf16[4,256,768]{2,1,0:T(8,128)(2,1)S(1)}, bf16[4,256,768]{2,1,0:T(8,128)(2,1)S(1)}) custom-call(bf16[4,256,768]{2,1,0:T(8,128)(2,1)} %bitcast.145, bf16[4,256,768]{2,1,0:T(8,128)(2,1)} %bitcast.144), custom_call_target="tpu_custom_call" | custom-call | tf_op jit(solution)/shard_map/dispatch_exchange/pallas_call | solution.py:365
  243.5 1.2 copy-done.5
  244.6 1.2 copy-done.6
  245.8 38.9 %experts.1 = (bf16[1024,768]{1,0:T(8,128)(2,1)S(1)}, bf16[1024,768]{1,0:T(8,128)(2,1)S(1)}, bf16[4,768,384]{2,1,0:T(8,128)(2,1)}, bf16[4,768,384]{2,1,0:T(8,128)...) custom-call(bf16[1024,768]{1,0:T(8,128)(2,1)} %bitcast.141, bf16[1024,768]{1,0:T(8,128)(2,1)} %bitcast.142, ...), custom_call_target="tpu_custom_call" | custom-call | flops 40000000000 | bytes 30000000 | tf_op jit(solution)/shard_map/experts/pallas_call | solution.py:590
  284.7 1.1 copy-done.3
  285.8 1.1 copy-done.4
  287.0 35.7 %return_exchange.1 = (bf16[4,256,768]{2,1,0:T(8,128)(2,1)S(1)}, bf16[4,256,768]{2,1,0:T(8,128)(2,1)S(1)}) custom-call(bf16[4,256,768]{2,1,0:T(8,128)(2,1)} %bitcast.133, bf16[4,256,768]{2,1,0:T(8,128)(2,1)} %bitcast.134), custom_call_target="tpu_custom_call" | custom-call | tf_op jit(solution)/shard_map/return_exchange/pallas_call | solution.py:365
  322.7 1.2 fusion.14
  325.3 1.9 multiply_reduce_fusion
  327.3 1.6 fusion.46
  328.9 1.4 fusion.45
  331.2 22.3 %d_attended_exchange.1 = bf16[4,256,384]{2,1,0:T(8,128)(2,1)S(1)} custom-call(bf16[2,2,256,384]{3,2,1,0:T(8,128)(2,1)S(1)} %fusion.21.t_ref), custom_call_target="tpu_custom_call" | custom-call | tf_op jit(solution)/shard_map/d_attended_exchange/pallas_call | solution.py:249
  353.5 20.4 %attention_backward.1 = (bf16[3,768,384]{2,1,0:T(8,128)(2,1)}, bf16[4,256,768]{2,1,0:T(8,128)(2,1)S(1)}) custom-call(s32[1]{0:T(128)} %bitcast.1.len_ref, bf16[1024,768]{1,0:T(8,128)(2,1)S(1)} %bitcast.132, bf16[768,1152]{1,0:T(8,128)(2,1)} %pad_maximum_fusion.w_ref, bf16[1024,1152]{1,0:T(8,128)(2,1)} %get-tuple-element.41.qkv_ref, f32[384,1024]{1,0:T(8,128)} %copy-done.7, ...), custom_call_target="tpu_custom_call" | custom-call | flops 40000000000 | bytes 10000000 | tf_op jit(solution)/shard_map/attention_backward/pallas_call | solution.py:519
  373.9 20.8 %d_normed_exchange.1 = bf16[2,2,128,768]{3,2,1,0:T(8,128)(2,1)S(1)} custom-call(bf16[4,2,128,768]{3,2,1,0:T(8,128)(2,1)S(1)} %bitcast.135), custom_call_target="tpu_custom_call" | custom-call | tf_op jit(solution)/shard_map/d_normed_exchange/pallas_call | solution.py:323
  395.9 1.1 convert_element_type.104
  396.9 0.9 fusion.10
  400.1 87.0 %dense_grad_sum.1 = (bf16[2,2,2,2,4,96,384]{6,5,4,3,2,1,0:T(8,128)(2,1)}, f32[16,768]{1,0:T(8,128)S(1)}) custom-call(bf16[3,768,384]{2,1,0:T(8,128)(2,1)S(1)} %copy-done.2, bf16[2,768,384]{2,1,0:T(8,128)(2,1)S(1)} %bitcast.138, f32[16,768]{1,0:T(8,128)S(1)} %pad.4.s_ref), custom_call_target="tpu_custom_call" | custom-call | tf_op jit(solution)/shard_map/dense_grad_sum/pallas_call | solution.py:836
  488.8 109.1 %expert_grad_sum.1 = (f32[768,384]{1,0:T(8,128)S(1)}, f32[384,768]{1,0:T(8,128)S(1)}) custom-call(bf16[4,768,384]{2,1,0:T(8,128)(2,1)} %get-tuple-element.48.gio_ref, bf16[4,768,384]{2,1,0:T(8,128)(2,1)} %get-tuple-element.49.gis_ref, bf16[4,384,768]{2,1,0:T(8,128)(2,1)} %get-tuple-element.50.goo_ref, bf16[4,384,768]{2,1,0:T(8,128)(2,1)} %get-tuple-element.51.gos_ref), custom_call_target="tpu_custom_call" | custom-call | tf_op jit(solution)/shard_map/expert_grad_sum/pallas_call | solution.py:668
  598.0 2.3 slice_bitcast_fusion.1
  601.6 2.9 maximum_convert_fusion.3
  604.5 1.6 maximum_convert_fusion.2
  606.2 1.6 maximum_convert_fusion.1
  607.8 1.6 maximum_convert_fusion
  609.4 0.9 copy-done.15
  610.4 1.7 add_add_fusion.2
  612.1 1.0 copy.55
  613.1 1.0 copy.56
  (148 shorter events, 20.0 us)
Async XLA Ops:
  7.2 141.9 %copy-start = (bf16[768,768]{1,0:T(8,128)(2,1)S(1)}, bf16[768,768]{1,0:T(8,128)(2,1)}, u32[]{:S(2)}) copy-start(bf16[768,768]{1,0:T(8,128)(2,1)} %param.20) | copy-start | bytes 3538948
  7.2 10.9 %copy-start.10 = (bf16[2,256,768]{2,1,0:T(8,128)(2,1)S(1)}, bf16[2,256,768]{2,1,0:T(8,128)(2,1)}, u32[]{:S(2)}) copy-start(bf16[2,256,768]{2,1,0:T(8,128)(2,1)} %param.15) | copy-start | bytes 2359300
  7.2 11.4 %copy-start.28 = (f32[768]{0:T(1024)S(1)}, f32[768]{0:T(1024)}, u32[]{:S(2)}) copy-start(f32[768]{0:T(1024)} %param.21) | copy-start | bytes 9220
  7.2 11.4 %copy-start.42 = (f32[768]{0:T(1024)S(1)}, f32[768]{0:T(1024)}, u32[]{:S(2)}) copy-start(f32[768]{0:T(1024)} %param.22) | copy-start | bytes 9220
  7.2 146.6 %all-gather.4.cloned.1.call-start = ((), (), s32[]{:S(2)}) async-start(), calls=%async_computation | async-start | bytes 2949120 | tf_op jit(solution)/shard_map/all_gather | solution.py:900
  8.0 145.9 %all-gather.6.cloned.1.call-start = ((), (), s32[]{:S(2)}) async-start(), calls=%async_computation.1 | async-start | bytes 2949120 | tf_op jit(solution)/shard_map/all_gather | solution.py:901
  78.2 2.1 copy-start.26
  101.8 1.1 copy-start.7
  102.9 0.6 copy-start.8
  103.6 38.5 %copy-start.45 = (s32[2]{0:T(128)S(1)}, s32[2]{0:T(128)}, u32[]{:S(2)}) copy-start(s32[2]{0:T(128)} %param.29) | copy-start | bytes 28
  103.6 39.2 %copy-start.27 = (s32[1,1,2,256,1]{3,4,2,1,0:T(1,128)S(1)}, s32[1,1,2,256,1]{3,4,2,1,0:T(1,128)}, u32[]{:S(2)}) copy-start(s32[1,1,2,256,1]{3,4,2,1,0:T(1,128)} %param.28) | copy-start | bytes 6148
  151.1 1.2 copy-start.13
  151.1 2.0 copy-start.39
  153.8 92.0 %collective-permute-start = (bf16[4,768,384]{2,1,0:T(8,128)(2,1)}, bf16[4,768,384]{2,1,0:T(8,128)(2,1)}, u32[]{:S(2)}, u32[]{:S(2)}) collective-permute-start(bf16[4,768,384]{2,1,0:T(8,128)(2,1)} %all-gather.4.cloned.1.call-done.io_ref), channel_id=1, source_target_pairs={{0,1},{1,0},{2,3},{3,2},{4,5},{5,4},{6,7},{7,6},{8,9},{9,8},{10,11... | collective-permute-start | bytes 7077896 | tf_op jit(solution)/shard_map/ppermute | solution.py:903
  153.8 92.0 %collective-permute-start.1 = (bf16[4,384,768]{2,1,0:T(8,128)(2,1)}, bf16[4,384,768]{2,1,0:T(8,128)(2,1)}, u32[]{:S(2)}, u32[]{:S(2)}) collective-permute-start(bf16[4,384,768]{2,1,0:T(8,128)(2,1)} %all-gather.6.cloned.1.call-done.oo_ref), channel_id=1, source_target_pairs={{0,1},{1,0},{2,3},{3,2},{4,5},{5,4},{6,7},{7,6},{8,9},{9,8},{10,11... | collective-permute-start | bytes 7077896 | tf_op jit(solution)/shard_map/ppermute | solution.py:904
  198.2 2.9 copy-start.41
  198.2 3.5 copy-start.16
  243.5 1.2 copy-start.5
  244.6 1.2 copy-start.6
  284.7 1.2 copy-start.3
  285.8 1.1 copy-start.4
  322.7 2.0 copy-start.33
  323.9 1.4 copy-start.14
  323.9 1.4 copy-start.38
  325.3 2.0 copy-start.37
  330.3 0.9 copy-start.17
  331.2 22.3 %copy-start.9 = (f32[6,1024]{1,0:T(8,128)S(1)}, f32[6,1024]{1,0:T(8,128)}, u32[]{:S(2)}) copy-start(f32[6,1024]{1,0:T(8,128)} %copy-done.8) | copy-start | bytes 73732
  373.9 20.8 %copy-start.11 = (bf16[2,256,768]{2,1,0:T(8,128)(2,1)S(1)}, bf16[2,256,768]{2,1,0:T(8,128)(2,1)}, u32[]{:S(2)}) copy-start(bf16[2,256,768]{2,1,0:T(8,128)(2,1)} %param.15) | copy-start | bytes 2359300
  373.9 20.8 %copy-start.29 = (f32[768]{0:T(1024)S(1)}, f32[768]{0:T(1024)}, u32[]{:S(2)}) copy-start(f32[768]{0:T(1024)} %param.21) | copy-start | bytes 9220
  394.7 1.1 copy-start.18
  395.2 1.7 copy-start.35
  395.2 1.7 copy-start.32
  395.8 2.0 copy-start.44
  395.8 2.1 copy-start.43
  395.9 2.7 copy-start.30
  396.9 1.7 copy-start.25
  398.6 1.5 copy-start.2
  488.8 109.1 %slice-start = ((s8[4718592]{0:T(1024)(128)(4,1)}), s8[4194304]{0:T(1024)(128)(4,1)S(1)}, s32[]{:S(2)}) async-start(s8[4718592]{0:T(1024)(128)(4,1)} %bitcast.147), calls=%async_computation.2 | async-start | bytes 8388608
  488.8 109.1 %slice-start.1 = ((s8[4718592]{0:T(1024)(128)(4,1)}), s8[524288]{0:T(1024)(128)(4,1)S(1)}, s32[]{:S(2)}) async-start(s8[4718592]{0:T(1024)(128)(4,1)} %bitcast.147), calls=%async_computation.3 | async-start | bytes 1048576
  601.6 2.9 copy-start.23
  601.6 2.9 copy-start.24
  604.5 1.6 copy-start.21
  604.5 1.6 copy-start.22
  606.2 1.6 copy-start.19
  606.2 1.7 copy-start.20
  607.8 1.6 copy-start.12
  607.8 2.5 copy-start.15
  612.1 2.0 copy-start.1
  (4 other events, 2.3 us)
Sparse Core Ops, SparseCore 0:
  9.6 64.6 all-gather.3
  75.9 65.7 all-gather.5

commit v2 on v1

v2 whole, which is shorter than its diff:
```python
import functools

import jax
import jax.numpy as jnp
from jax import lax
from jax.experimental import pallas as pl
from jax.experimental.pallas import tpu as pltpu
from jax.sharding import PartitionSpec as P

HEAD = 64
MESH = pl.DeviceIdType.MESH
ANY = pl.BlockSpec(memory_space=pl.ANY)
VMEM = pl.BlockSpec(memory_space=pltpu.VMEM)
SMEM = pl.BlockSpec(memory_space=pltpu.SMEM)
DMA = pltpu.SemaphoreType.DMA
f32 = jnp.float32
bf16 = jnp.bfloat16

epsilon = 1e-05
balance_weight = 6.0
masked_fill = -1e30
VMEM_BYTES = 50 * 1024 * 1024


def dot(a, b):
    return lax.dot_general(a, b, (((1,), (0,)), ((), ())), preferred_element_type=f32)


def dot_nt(a, b):
    return lax.dot_general(a, b, (((1,), (1,)), ((), ())), preferred_element_type=f32)


def dot_tn(a, b):
    return lax.dot_general(a, b, (((0,), (0,)), ((), ())), preferred_element_type=f32)


def place():
    z = lax.axis_index("blk")
    e = lax.axis_index("ep")
    c = lax.rem(e, 2)
    return z, e, c, e - c


def remote(src, dst, send_sem, recv_sem, z, e):
    return pltpu.make_async_remote_copy(
        src, dst, send_sem, recv_sem, device_id=(z, e), device_id_type=MESH
    )


def greet(partners):
    barrier = pltpu.get_barrier_semaphore()
    for z, e in partners:
        pl.semaphore_signal(barrier, inc=1, device_id=(z, e), device_id_type=MESH)
    pl.semaphore_wait(barrier, len(partners))


def column_partners(blocks, z, c, base):
    found = [(z, base + 1 - c)]
    for step in range(1, blocks):
        for k in range(2):
            found.append((lax.rem(z + step, blocks), base + k))
    return found


def params(collective_id):
    return pltpu.CompilerParams(
        collective_id=collective_id, has_side_effects=True, vmem_limit_bytes=VMEM_BYTES
    )


def normed_exchange(normed, blocks):
    seqs, span, width = normed.shape
    half = span // 2

    def kernel(n_ref, x_ref, loc_sem, send_sem, recv_sem, fsend_sem, frecv_sem):
        z, e, c, base = place()
        seq_core = z // 2
        greet(column_partners(blocks, z, c, base))

        def outgoing(s, k):
            return remote(
                n_ref.at[s, k], x_ref.at[z, k], send_sem.at[s, k], recv_sem.at[z], 2 * c + s, base + k
            )

        def own(s, k):
            return pltpu.make_async_copy(n_ref.at[s, k], x_ref.at[z, k], loc_sem)

        for s in range(seqs):
            for k in range(2):
                to_self = (2 * c + s == z) & (c == k)

                @pl.when(to_self)
                def _():
                    own(s, k).start()

                @pl.when(jnp.logical_not(to_self))
                def _():
                    outgoing(s, k).start()

        def forward(zs):
            return remote(
                x_ref.at[zs, c], x_ref.at[zs, c], fsend_sem.at[zs], frecv_sem.at[zs], z, base + 1 - c
            )

        for step in range(blocks):
            zs = lax.rem(z + step, blocks)
            if step == 0:

                @pl.when(c == seq_core)
                def _():
                    pltpu.make_async_copy(n_ref.at[0, 0], x_ref.at[z, c], loc_sem).wait()

                @pl.when(c != seq_core)
                def _():
                    remote(n_ref.at[0, 0], x_ref.at[z, c], send_sem.at[0, 0], recv_sem.at[z], z, base).wait_recv()
            else:
                remote(n_ref.at[0, 0], x_ref.at[zs, c], send_sem.at[0, 0], recv_sem.at[zs], z, base).wait_recv()
            forward(zs).start()
        for step in range(blocks):
            zs = lax.rem(z + step, blocks)
            forward(zs).wait_send()
            remote(
                x_ref.at[zs, 1 - c], x_ref.at[zs, 1 - c], fsend_sem.at[zs], frecv_sem.at[zs], z, base + 1 - c
            ).wait_recv()
        for s in range(seqs):
            for k in range(2):

                @pl.when(jnp.logical_not((2 * c + s == z) & (c == k)))
                def _():
                    outgoing(s, k).wait_send()

    return pl.pallas_call(
        kernel,
        name="normed_exchange",
        out_shape=jax.ShapeDtypeStruct((blocks, 2, half, width), bf16),
        in_specs=[ANY],
        out_specs=ANY,
        scratch_shapes=[DMA, DMA((seqs, 2)), DMA((blocks,)), DMA((blocks,)), DMA((blocks,))],
        compiler_params=params(1),
    )(normed.reshape(seqs, 2, half, width)).reshape(blocks * span, width)


def attended_exchange(att, blocks):
    _, span, width = att.shape
    seqs = 2

    def kernel(a_ref, t_ref, loc_sem, send_sem, recv_sem):
        z, e, c, base = place()
        seq_core, seq = z // 2, lax.rem(z, 2)
        greet(column_partners(blocks, z, c, base))

        def outgoing(j):
            return remote(
                a_ref.at[j], t_ref.at[seq, c], send_sem.at[j], recv_sem.at[seq, c], j, base + seq_core
            )

        def own():
            return pltpu.make_async_copy(a_ref.at[z], t_ref.at[seq, c], loc_sem)

        for step in range(1, blocks):
            outgoing(lax.rem(z + step, blocks)).start()

        @pl.when(seq_core == c)
        def _():
            own().start()

        @pl.when(seq_core != c)
        def _():
            outgoing(z).start()

        for s in range(seqs):
            for k in range(2):
                from_self = (2 * c + s == z) & (c == k)

                @pl.when(jnp.logical_not(from_self))
                def _():
                    remote(a_ref.at[0], t_ref.at[s, k], send_sem.at[0], recv_sem.at[s, k], z, base).wait_recv()

        for step in range(1, blocks):
            outgoing(lax.rem(z + step, blocks)).wait_send()

        @pl.when(seq_core == c)
        def _():
            own().wait()

        @pl.when(seq_core != c)
        def _():
            outgoing(z).wait_send()

    return pl.pallas_call(
        kernel,
        name="attended_exchange",
        out_shape=jax.ShapeDtypeStruct((seqs, 2, span, width), bf16),
        in_specs=[ANY],
        out_specs=ANY,
        scratch_shapes=[DMA, DMA((blocks,)), DMA((seqs, 2))],
        compiler_params=params(2),
    )(att)


def plane_exchange(arrays, columns, collective_id, name):
    count = len(arrays)

    def kernel(*refs):
        sources, targets = refs[:count], refs[count : 2 * count]
        loc_sem, send_sem, recv_sem = refs[2 * count :]
        z, e, c, base = place()
        col = e // 2
        others = [lax.rem(col + step, columns) for step in range(1, columns)]
        greet([(z, 2 * t + c) for t in others])
        for i in range(count):
            for t in others:
                remote(
                    sources[i].at[t], targets[i].at[col], send_sem.at[i, t], recv_sem.at[i, col], z, 2 * t + c
                ).start()
            pltpu.make_async_copy(sources[i].at[col], targets[i].at[col], loc_sem.at[i]).start()
        for i in range(count):
            pltpu.make_async_copy(sources[i].at[col], targets[i].at[col], loc_sem.at[i]).wait()
            for t in others:
                remote(
                    sources[i].at[t], targets[i].at[t], send_sem.at[i, t], recv_sem.at[i, t], z, 2 * t + c
                ).wait()

    return pl.pallas_call(
        kernel,
        name=name,
        out_shape=[jax.ShapeDtypeStruct(a.shape, a.dtype) for a in arrays],
        in_specs=[ANY] * count,
        out_specs=[ANY] * count,
        scratch_shapes=[DMA((count,)), DMA((count, columns)), DMA((count, columns))],
        compiler_params=params(collective_id),
    )(*arrays)


def attention_forward(length, rows, weights, span):
    total, width = rows.shape
    half = weights.shape[1] // 3
    pairs = half // 128
    blocks = total // span

    def kernel(len_ref, x_ref, w_ref, qkv_ref, att_ref, attt_ref, lse_ref, vt_ref):
        seq_len = len_ref[0]
        for j in range(blocks):
            r = pl.ds(j * span, span)
            qkv_ref[r, :] = dot(x_ref[r, :], w_ref[...]).astype(bf16)
        lane = lax.broadcasted_iota(jnp.int32, (1, 128), 1)
        key_place = lax.broadcasted_iota(jnp.int32, (total, 1), 0)
        key_bias = jnp.where(key_place < seq_len, 0.0, masked_fill)
        later = lax.broadcasted_iota(jnp.int32, (span, span), 0) > lax.broadcasted_iota(
            jnp.int32, (span, span), 1
        )

        def pair_step(p, _):
            first = pl.multiple_of(p * 128, 128)
            k_all = qkv_ref[:, pl.ds(half + first, 128)]
            vt_ref[...] = jnp.transpose(qkv_ref[:, pl.ds(2 * half + first, 128)])
            k_heads = []
            for h in range(2):
                inside = (lane // HEAD) == h
                spare = lane == (1 - h) * HEAD
                k_heads.append(
                    jnp.where(
                        inside, k_all.astype(f32), jnp.where(spare, key_bias, 0.0)
                    ).astype(bf16)
                )
            for j in range(blocks):
                n = (j + 1) * span
                r = pl.ds(j * span, span)
                q = qkv_ref[r, pl.ds(first, 128)].astype(f32) * (HEAD**-0.5)
                out_t = []
                for h in range(2):
                    inside = (lane // HEAD) == h
                    spare = lane == (1 - h) * HEAD
                    q_h = jnp.where(inside, q, jnp.where(spare, 1.0, 0.0)).astype(bf16)
                    s = dot_nt(k_heads[h][:n], q_h)
                    last = jnp.where(later, masked_fill, s[n - span :])
                    s = last if j == 0 else jnp.concatenate([s[: n - span], last], axis=0)
                    top = jnp.max(s, axis=0, keepdims=True)
                    w = jnp.exp(s - top)
                    total_w = jnp.sum(w, axis=0, keepdims=True)
                    o_t = dot(vt_ref[h * HEAD : (h + 1) * HEAD, :n], w.astype(bf16))
                    out_t.append(o_t / total_w)
                    lse_ref[pl.ds(2 * p + h, 1), r] = top + jnp.log(total_w)
                o = jnp.concatenate(out_t, axis=0)
                attt_ref[pl.ds(first, 128), r] = o
                att_ref[j, :, pl.ds(first, 128)] = jnp.transpose(o).astype(bf16)
            return 0

        lax.fori_loop(0, pairs, pair_step, 0)

    return pl.pallas_call(
        kernel,
        name="attention_forward",
        out_shape=[
            jax.ShapeDtypeStruct((total, 3 * half), bf16),
            jax.ShapeDtypeStruct((blocks, span, half), bf16),
            jax.ShapeDtypeStruct((half, total), f32),
            jax.ShapeDtypeStruct((2 * pairs, total), f32),
        ],
        in_specs=[SMEM, VMEM, VMEM],
        out_specs=[VMEM] * 4,
        scratch_shapes=[pltpu.VMEM((128, total), bf16)],
        compiler_params=pltpu.CompilerParams(vmem_limit_bytes=VMEM_BYTES),
        cost_estimate=pl.CostEstimate(flops=20 * 10**9, bytes_accessed=10**7, transcendentals=0),
    )(length, rows, weights)


def experts(rows, d_out, inner_own, inner_sib, outer_own, outer_sib):
    total, width = rows.shape
    steps, _, part = inner_own.shape
    block = 256

    def kernel(
        x_ref, d_ref, io_ref, is_ref, oo_ref, os_ref,
        out_ref, dx_ref, gio_ref, gis_ref, goo_ref, gos_ref,
        oacc_ref, dacc_ref, act_ref, dpre_ref, wi_ref, wo_ref,
    ):
        g = pl.program_id(0)
        wi_ref[:, :part] = io_ref[0]
        wi_ref[:, part:] = is_ref[0]
        wo_ref[:part] = oo_ref[0]
        wo_ref[part:] = os_ref[0]

        @pl.when(g == 0)
        def _():
            oacc_ref[...] = jnp.zeros_like(oacc_ref)
            dacc_ref[...] = jnp.zeros_like(dacc_ref)

        def row_step(b, _):
            r = pl.ds(pl.multiple_of(b * block, block), block)
            pre = dot(x_ref[r, :], wi_ref[...])
            cdf = 0.5 * (1.0 + lax.erf(pre * (0.5**0.5)))
            act = (pre * cdf).astype(bf16)
            slope = cdf + pre * (jnp.exp(-0.5 * pre * pre) * ((2 * jnp.pi) ** -0.5))
            d_act = dot_nt(d_ref[r, :], wo_ref[...])
            d_pre = (d_act * slope).astype(bf16)
            act_ref[r, :] = act
            dpre_ref[r, :] = d_pre
            oacc_ref[r, :] += dot(act, wo_ref[...])
            dacc_ref[r, :] += dot_nt(d_pre, wi_ref[...])
            return 0

        lax.fori_loop(0, total // block, row_step, 0)
        g_inner = dot_tn(x_ref[...], dpre_ref[...]).astype(bf16)
        gio_ref[0] = g_inner[:, :part]
        gis_ref[0] = g_inner[:, part:]
        g_outer = dot_tn(act_ref[...], d_ref[...]).astype(bf16)
        goo_ref[0] = g_outer[:part]
        gos_ref[0] = g_outer[part:]

        @pl.when(g == steps - 1)
        def _():
            out_ref[...] = oacc_ref[...].astype(bf16)
            dx_ref[...] = dacc_ref[...].astype(bf16)

    whole = pl.BlockSpec((total, width), lambda g: (0, 0))
    inner = pl.BlockSpec((1, width, part), lambda g: (g, 0, 0))
    outer = pl.BlockSpec((1, part, width), lambda g: (g, 0, 0))
    return pl.pallas_call(
        kernel,
        name="experts",
        grid=(steps,),
        out_shape=[
            jax.ShapeDtypeStruct((total, width), bf16),
            jax.ShapeDtypeStruct((total, width), bf16),
            jax.ShapeDtypeStruct((steps, width, part), bf16),
            jax.ShapeDtypeStruct((steps, width, part), bf16),
            jax.ShapeDtypeStruct((steps, part, width), bf16),
            jax.ShapeDtypeStruct((steps, part, width), bf16),
        ],
        in_specs=[whole, whole, inner, inner, outer, outer],
        out_specs=[whole, whole, inner, inner, outer, outer],
        scratch_shapes=[
            pltpu.VMEM((total, width), f32),
            pltpu.VMEM((total, width), f32),
            pltpu.VMEM((total, 2 * part), bf16),
            pltpu.VMEM((total, 2 * part), bf16),
            pltpu.VMEM((width, 2 * part), bf16),
            pltpu.VMEM((2 * part, width), bf16),
        ],
        compiler_params=pltpu.CompilerParams(
            vmem_limit_bytes=VMEM_BYTES, dimension_semantics=("arbitrary",)
        ),
        cost_estimate=pl.CostEstimate(flops=40 * 10**9, bytes_accessed=3 * 10**7, transcendentals=0),
    )(rows, d_out, inner_own, inner_sib, outer_own, outer_sib)


class PieceSum:
    def __init__(self, at, part, got1, got2, got3, gotr, full, sem, rsem, zsem, zrsem, order):
        self.at, self.part, self.full = at, part, full
        self.got1, self.got2, self.got3, self.gotr = got1, got2, got3, gotr
        self.sem, self.rsem, self.zsem, self.zrsem = sem, rsem, zsem, zrsem
        z, e, c, bit, mate, blocks, sib = at
        self.first, self.second = order
        self.rest = len(bit) - 2

    def swap(self, n, src, dst, e):
        return remote(src, dst, self.sem.at[n], self.rsem.at[n], self.at[0], e)

    def halves(self):
        z, e, c, bit, mate, blocks, sib = self.at
        return self.swap(0, self.part.at[1 - bit[self.first]], self.got1, mate[self.first])

    def quarters(self):
        z, e, c, bit, mate, blocks, sib = self.at
        b1, b2 = bit[self.first], bit[self.second]
        return self.swap(1, self.part.at[b1, 1 - b2], self.got2, mate[self.second])

    def to_z(self, zt):
        z, e, c, bit, mate, blocks, sib = self.at
        b1, b2 = bit[self.first], bit[self.second]
        return remote(
            self.part.at[b1, b2, zt], self.got3.at[z], self.zsem.at[0, zt], self.zrsem.at[0, z], zt, e
        )

    def own(self):
        z, e, c, bit, mate, blocks, sib = self.at
        return self.full.at[c, bit[self.first], bit[self.second], z]

    def back_z(self, zt):
        z, e, c, bit, mate, blocks, sib = self.at
        return remote(self.own(), self.own(), self.zsem.at[1, zt], self.zrsem.at[1, z], zt, e)

    def back_quarter(self):
        z, e, c, bit, mate, blocks, sib = self.at
        at = self.full.at[c, bit[self.first], bit[self.second]]
        return self.swap(2, at, at, mate[self.second])

    def back_half(self):
        z, e, c, bit, mate, blocks, sib = self.at
        at = self.full.at[c, bit[self.first]]
        return self.swap(3, at, at, mate[self.first])

    def to_sibling(self):
        z, e, c, bit, mate, blocks, sib = self.at
        return self.swap(4, self.full.at[c], self.full.at[c], sib)

    def step(self, n):
        z, e, c, bit, mate, blocks, sib = self.at
        b1, b2 = bit[self.first], bit[self.second]
        others = [lax.rem(z + step, blocks) for step in range(1, blocks)]
        if n == 0:
            self.halves().start()
        elif n == 1:
            self.halves().wait()
            self.part[b1] = (self.part[b1].astype(f32) + self.got1[...].astype(f32)).astype(bf16)
            self.quarters().start()
        elif n == 2:
            self.quarters().wait()
            self.part[b1, b2] = (self.part[b1, b2].astype(f32) + self.got2[...].astype(f32)).astype(bf16)
            for zt in others:
                self.to_z(zt).start()
        elif n == 3:
            for zs in others:
                remote(
                    self.got3.at[0], self.got3.at[zs], self.zsem.at[0, zs], self.zrsem.at[0, zs], z, e
                ).wait_recv()
            for zt in others:
                self.to_z(zt).wait_send()
            self.got3[z] = self.part[b1, b2, z]
            total = self.got3[0].astype(f32)
            for j in range(1, blocks):
                total = total + self.got3[j].astype(f32)
            own = self.own()
            own[...] = total.astype(bf16)
            for r in range(self.rest):
                copy = self.swap(5 + r, own, self.gotr.at[r], mate[2 + r])
                copy.start()
                copy.wait()
                own[...] = (own[...].astype(f32) + self.gotr[r].astype(f32)).astype(bf16)
            for zt in others:
                self.back_z(zt).start()
        elif n == 4:
            for zs in others:
                at = self.full.at[c, b1, b2, zs]
                remote(at, at, self.zsem.at[1, zs], self.zrsem.at[1, zs], z, e).wait_recv()
            for zt in others:
                self.back_z(zt).wait_send()
            self.back_quarter().start()
        elif n == 5:
            self.back_quarter().wait()
            self.back_half().start()
        elif n == 6:
            self.back_half().wait()
            self.to_sibling().start()
        elif n == 7:
            self.to_sibling().wait()

    @staticmethod
    def scratch(blocks, piece, lanes, rest):
        return [
            pltpu.VMEM((2, 2, blocks, piece, lanes), bf16),
            pltpu.VMEM((2, blocks, piece, lanes), bf16),
            pltpu.VMEM((blocks, piece, lanes), bf16),
            pltpu.VMEM((blocks, piece, lanes), bf16),
            pltpu.VMEM((max(1, rest), piece, lanes), bf16),
            DMA((5 + rest,)),
            DMA((5 + rest,)),
            DMA((2, blocks)),
            DMA((2, blocks)),
        ]


def backward(
    length, rows, weights, qkv, att_t, lse, d_attended, out_part, small, hidden, gain, d_middle,
    gi_own, gi_sib, go_own, go_sib, span, columns,
):
    total, width = rows.shape
    half = weights.shape[1] // 3
    pairs = half // 128
    blocks = total // span
    seqs = d_attended.shape[0]
    hs = span // 2
    scale = HEAD**-0.5
    part = gi_own.shape[2]
    bits = columns.bit_length() - 1
    assert columns == 1 << bits and bits >= 2
    rest = bits - 2
    small_rows = small.shape[0]
    out_piece, pair_piece = width // (4 * blocks), 3 * width // (4 * blocks)
    n_sum = 9

    def kernel(*refs):
        (
            len_ref, x_ref, w_ref, qkv_ref, attt_ref, lse_ref, datt_ref, op_ref, small_ref, hid_ref, gain_ref, dmid_ref,
            gio_ref, gis_ref, goo_ref, gos_ref,
        ) = refs[:16]
        gout_ref, gpair_ref, sums_ref, fi_ref, fo_ref, gh_ref = refs[16:22]
        (
            do_ref, dqkv_ref, kt_ref, dk_ref, dv_ref, xt_ref, dn_ref, dsib_ref, dsum_ref, dnt_ref,
            oi, oo, si, so, zi, zo, osib, sgot, szgot,
            loc_sem, dsend, drecv, rloc, rssend, rsrecv, rsend, rrecv,
            nsend, nrecv, ssend, srecv, osend, orecv, tsend, trecv, tzsend, tzrecv,
        ) = refs[22:59]
        sums_scratch = refs[59:]
        z, e, c, base = place()
        col = e // 2
        sib = base + 1 - c
        seq_core, seq = z // 2, lax.rem(z, 2)
        bit = [lax.rem(col // (1 << i), 2) for i in range(bits)]
        mate = [2 * (col + (1 - 2 * bit[i]) * (1 << i)) + c for i in range(bits)]
        others = [lax.rem(z + step, blocks) for step in range(1, blocks)]
        greet(column_partners(blocks, z, c, base) + [(z, mate[i]) for i in range(bits)])

        at = (z, e, c, bit, mate, blocks, sib)
        out_sum = PieceSum(at, *sums_scratch[0:5], gout_ref, *sums_scratch[5:9], (0, 1))
        pair_sums = [
            PieceSum(
                at,
                *sums_scratch[n_sum * (p + 1) : n_sum * (p + 1) + 5],
                gpair_ref.at[p],
                *sums_scratch[n_sum * (p + 1) + 5 : n_sum * (p + 2)],
                (1, 0) if p % 2 == 0 else (0, 1),
            )
            for p in range(pairs)
        ]

        def d_out(s, k):
            return remote(
                datt_ref.at[s, k], do_ref.at[z], dsend.at[s, k], drecv.at[z], 2 * c + s, base + k
            )

        def d_own(s, k):
            return pltpu.make_async_copy(datt_ref.at[s, k], do_ref.at[z], loc_sem.at[0])

        for s in range(seqs):
            for k in range(2):
                to_self = (2 * c + s == z) & (c == k)

                @pl.when(to_self)
                def _():
                    d_own(s, k).start()

                @pl.when(jnp.logical_not(to_self))
                def _():
                    d_out(s, k).start()

        r_order = others[1:2] + others[0:1] + others[2:] + [z]
        kinds = ((0, gio_ref, gis_ref, oi, si, zi, fi_ref), (1, goo_ref, gos_ref, oo, so, zo, fo_ref))

        def r_sib(i, src, dst, j):
            return remote(src.at[j], dst.at[j], rssend.at[i, j], rsrecv.at[i, j], z, sib)

        def r_loc(i, src, dst, j):
            return pltpu.make_async_copy(src.at[j], dst.at[j], rloc.at[i, j])

        def r_z(i, src, dst, j):
            return remote(src.at[j], dst.at[z], rsend.at[i, j], rrecv.at[i, z], j, e)

        o_first = remote(op_ref.at[1 - c], osib, osend, orecv, z, sib)
        o_first.start()
        for j in r_order:
            for i, own, sibs, own_buf, sib_buf, z_buf, final in kinds:
                r_sib(i, sibs, sib_buf, j).start()
                r_loc(i, own, own_buf, j).start()

        xt_ref[...] = jnp.transpose(x_ref[...])
        o_first.wait()
        out_sum.part[...] = (op_ref[c].astype(f32) + osib[...].astype(f32)).astype(bf16).reshape(
            2, 2, blocks, out_piece, half
        )
        out_sum.step(0)
        for n, j in enumerate(r_order):
            for i, own, sibs, own_buf, sib_buf, z_buf, final in kinds:
                r_loc(i, own, own_buf, j).wait()
                r_sib(i, sibs, sib_buf, j).wait_recv()
                own_buf[j] = (own_buf[j].astype(f32) + sib_buf[j].astype(f32)).astype(bf16)

        @pl.when(c == seq_core)
        def _():
            d_own(0, 0).wait()

        @pl.when(c != seq_core)
        def _():
            remote(datt_ref.at[0, 0], do_ref.at[z], dsend.at[0, 0], drecv.at[z], z, base).wait_recv()

        for zs in others:
            remote(datt_ref.at[0, 0], do_ref.at[zs], dsend.at[0, 0], drecv.at[zs], z, base).wait_recv()

        for j in r_order[:-1]:
            for i, own, sibs, own_buf, sib_buf, z_buf, final in kinds:
                r_z(i, own_buf, z_buf, j).start()

        seq_len = len_ref[0]
        lane = lax.broadcasted_iota(jnp.int32, (1, 128), 1)
        key_place = lax.broadcasted_iota(jnp.int32, (total, 1), 0)
        key_bias = jnp.where(key_place < seq_len, 0.0, masked_fill)
        later = lax.broadcasted_iota(jnp.int32, (span, span), 0) > lax.broadcasted_iota(
            jnp.int32, (span, span), 1
        )

        def pair_step(p):
            first = p * 128
            k_all = qkv_ref[:, pl.ds(half + first, 128)]
            kt_ref[...] = jnp.transpose(k_all)
            v_all = qkv_ref[:, pl.ds(2 * half + first, 128)]
            k_heads = []
            for h in range(2):
                inside = (lane // HEAD) == h
                spare = lane == (1 - h) * HEAD
                k_heads.append(
                    jnp.where(
                        inside, k_all.astype(f32), jnp.where(spare, key_bias, 0.0)
                    ).astype(bf16)
                )
            dk_ref[...] = jnp.zeros_like(dk_ref)
            dv_ref[...] = jnp.zeros_like(dv_ref)
            for j in range(blocks):
                n = (j + 1) * span
                r = pl.ds(j * span, span)
                q = qkv_ref[r, pl.ds(first, 128)].astype(f32) * scale
                d_o = do_ref[j, :, pl.ds(first, 128)].astype(f32)
                prod_t = jnp.transpose(d_o) * attt_ref[pl.ds(first, 128), r]
                dq_t = []
                for h in range(2):
                    inside = (lane // HEAD) == h
                    spare = lane == (1 - h) * HEAD
                    q_h = jnp.where(inside, q, jnp.where(spare, 1.0, 0.0)).astype(bf16)
                    q_only = jnp.where(inside, q, 0.0).astype(bf16)
                    do_h = jnp.where(inside, d_o, 0.0).astype(bf16)
                    delta = jnp.sum(prod_t[h * HEAD : (h + 1) * HEAD], axis=0, keepdims=True)
                    s = dot_nt(k_heads[h][:n], q_h)
                    last = jnp.where(later, masked_fill, s[n - span :])
                    s = last if j == 0 else jnp.concatenate([s[: n - span], last], axis=0)
                    w = jnp.exp(s - lse_ref[pl.ds(2 * p + h, 1), r])
                    d_w = dot_nt(v_all[:n], do_h)
                    d_s = (w * (d_w - delta)).astype(bf16)
                    dv_ref[:n] += dot(w.astype(bf16), do_h)
                    dk_ref[:n] += dot(d_s, q_only)
                    dq_t.append(dot(kt_ref[h * HEAD : (h + 1) * HEAD, :n], d_s))
                dq = jnp.transpose(jnp.concatenate(dq_t, axis=0)) * scale
                dqkv_ref[r, pl.ds(first, 128)] = dq.astype(bf16)
            dqkv_ref[:, pl.ds(half + first, 128)] = dk_ref[...].astype(bf16)
            dqkv_ref[:, pl.ds(2 * half + first, 128)] = dv_ref[...].astype(bf16)
            joined = jnp.concatenate(
                [dqkv_ref[:, pl.ds(m * half + first, 128)] for m in range(3)], axis=1
            )
            grads = dot(xt_ref[...], joined).astype(bf16)
            pair_sums[p].part[...] = jnp.concatenate(
                [grads[:, m * 128 : (m + 1) * 128] for m in range(3)], axis=0
            ).reshape(2, 2, blocks, pair_piece, 128)

        todo = [(out_sum, 1)]
        for p in range(pairs):
            pair_step(p)
            nexts = []
            for one, n in todo:
                one.step(n)
                if n < 7:
                    nexts.append((one, n + 1))
            pair_sums[p].step(0)
            todo = nexts + [(pair_sums[p], 1)]

        for j in range(blocks):
            r = pl.ds(j * span, span)
            dn_ref[j] = dot_nt(dqkv_ref[r, :], w_ref[...]).astype(bf16).reshape(2, hs, width)

        def n_sib(j):
            return remote(dn_ref.at[j, 1 - c], dsib_ref.at[j], nsend.at[j], nrecv.at[j], z, sib)

        def n_out(j):
            return remote(
                dsum_ref.at[j], dnt_ref.at[seq, c], ssend.at[j], srecv.at[seq, c], j, base + seq_core
            )

        def n_own():
            return pltpu.make_async_copy(dsum_ref.at[z], dnt_ref.at[seq, c], loc_sem.at[1])

        n_order = others[1:2] + others[0:1] + others[2:] + [z]
        for j in n_order:
            n_sib(j).start()
        for i, j in enumerate(n_order):
            n_sib(j).wait_recv()
            dsum_ref[j] = (dn_ref[j, c].astype(f32) + dsib_ref[j].astype(f32)).astype(bf16)
            if i < blocks - 1:
                n_out(j).start()
            else:

                @pl.when(seq_core == c)
                def _():
                    n_own().start()

                @pl.when(seq_core != c)
                def _():
                    n_out(j).start()

        def advance():
            nexts = []
            for one, n in todo:
                one.step(n)
                if n < 7:
                    nexts.append((one, n + 1))
            todo[:] = nexts

        advance()
        for s in range(seqs):
            for k in range(2):
                from_self = (2 * c + s == z) & (c == k)

                @pl.when(jnp.logical_not(from_self))
                def _():
                    remote(
                        dsum_ref.at[0], dnt_ref.at[s, k], ssend.at[0], srecv.at[s, k], z, base
                    ).wait_recv()

                @pl.when(from_self)
                def _():
                    n_own().wait()

        gains = gain_ref[...]
        gain_sum = jnp.zeros((1, width), f32)
        shift_sum = jnp.zeros((1, width), f32)
        for s in range(seqs):
            for k in range(2):
                v = hid_ref[s, k].astype(f32)
                centered = v - jnp.mean(v, axis=-1, keepdims=True)
                inverse = lax.rsqrt(jnp.mean(centered * centered, axis=-1, keepdims=True) + epsilon)
                unit = centered * inverse
                dy = dnt_ref[s, k].astype(f32)
                gain_sum = gain_sum + jnp.sum(dy * unit, axis=0, keepdims=True)
                shift_sum = shift_sum + jnp.sum(dy, axis=0, keepdims=True)
                du = dy * gains
                dx = inverse * (
                    du
                    - jnp.mean(du, axis=-1, keepdims=True)
                    - unit * jnp.mean(du * unit, axis=-1, keepdims=True)
                )
                gh_ref[s, k] = dmid_ref[s, k] + dx

        sums_ref[...] = small_ref[...]
        sums_ref[0:1] = gain_sum
        sums_ref[1:2] = shift_sum

        def t_swap(n, te):
            return remote(sums_ref, sgot.at[n], tsend.at[n], trecv.at[n], z, te)

        partners = [sib] + mate
        for n, te in enumerate(partners):
            copy = t_swap(n, te)
            copy.start()
            if n in (1, 2):
                advance()
            copy.wait()
            sums_ref[...] = sums_ref[...] + sgot[n]

        def t_z(zt):
            return remote(sums_ref, szgot.at[z], tzsend.at[zt], tzrecv.at[z], zt, e)

        for zt in others:
            t_z(zt).start()
        advance()
        for zs in others:
            remote(sums_ref, szgot.at[zs], tzsend.at[zs], tzrecv.at[zs], z, e).wait_recv()
        for zt in others:
            t_z(zt).wait_send()
        szgot[z] = sums_ref[...]
        tot = szgot[0]
        for j in range(1, blocks):
            tot = tot + szgot[j]
        sums_ref[...] = tot

        advance()
        for i, own, sibs, own_buf, sib_buf, z_buf, final in kinds:
            for zs in others:
                remote(own_buf.at[0], z_buf.at[zs], rsend.at[i, 0], rrecv.at[i, zs], z, e).wait_recv()
            z_buf[z] = own_buf[z]
            acc = z_buf[0].astype(f32)
            for j in range(1, blocks):
                acc = acc + z_buf[j].astype(f32)
            final[...] = acc
            advance()
        while todo:
            advance()

        for s in range(seqs):
            for k in range(2):

                @pl.when(jnp.logical_not((2 * c + s == z) & (c == k)))
                def _():
                    d_out(s, k).wait_send()

        for j in n_order[:-1]:
            n_out(j).wait_send()

        @pl.when(seq_core != c)
        def _():
            n_out(z).wait_send()

        for j in n_order:
            n_sib(j).wait_send()
            for i, own, sibs, own_buf, sib_buf, z_buf, final in kinds:
                r_sib(i, sibs, sib_buf, j).wait_send()
        for j in r_order[:-1]:
            for i, own, sibs, own_buf, sib_buf, z_buf, final in kinds:
                r_z(i, own_buf, z_buf, j).wait_send()

    stage = blocks
    scratch = [
        pltpu.VMEM((blocks, span, half), bf16),
        pltpu.VMEM((total, 3 * half), bf16),
        pltpu.VMEM((128, total), bf16),
        pltpu.VMEM((total, 128), f32),
        pltpu.VMEM((total, 128), f32),
        pltpu.VMEM((width, total), bf16),
        pltpu.VMEM((blocks, 2, hs, width), bf16),
        pltpu.VMEM((blocks, hs, width), bf16),
        pltpu.VMEM((blocks, hs, width), bf16),
        pltpu.VMEM((seqs, 2, hs, width), bf16),
        pltpu.VMEM((blocks, width, part), bf16),
        pltpu.VMEM((blocks, part, width), bf16),
        pltpu.VMEM((blocks, width, part), bf16),
        pltpu.VMEM((blocks, part, width), bf16),
        pltpu.VMEM((blocks, width, part), bf16),
        pltpu.VMEM((blocks, part, width), bf16),
        pltpu.VMEM((width, half), bf16),
        pltpu.VMEM((1 + bits, small_rows, width), f32),
        pltpu.VMEM((blocks, small_rows, width), f32),
        DMA((2,)),
        DMA((seqs, 2)),
        DMA((stage,)),
        DMA((2, stage)),
        DMA((2, stage)),
        DMA((2, stage)),
        DMA((2, stage)),
        DMA((2, stage)),
        DMA((stage,)),
        DMA((stage,)),
        DMA((stage,)),
        DMA((seqs, 2)),
        DMA,
        DMA,
        DMA((1 + bits,)),
        DMA((1 + bits,)),
        DMA((stage,)),
        DMA((stage,)),
    ]
    scratch += PieceSum.scratch(blocks, out_piece, half, rest)
    for _ in range(pairs):
        scratch += PieceSum.scratch(blocks, pair_piece, 128, rest)
    gout, gpair, sums, g_inner, g_outer, g_hidden = pl.pallas_call(
        kernel,
        name="backward",
        out_shape=[
            jax.ShapeDtypeStruct((2, 2, 2, blocks, out_piece, half), bf16),
            jax.ShapeDtypeStruct((pairs, 2, 2, 2, blocks, pair_piece, 128), bf16),
            jax.ShapeDtypeStruct(small.shape, f32),
            jax.ShapeDtypeStruct((width, part), f32),
            jax.ShapeDtypeStruct((part, width), f32),
            jax.ShapeDtypeStruct((seqs, 2, hs, width), f32),
        ],
        in_specs=[SMEM] + [VMEM] * 11 + [ANY] * 4,
        out_specs=[VMEM] * 6,
        scratch_shapes=scratch,
        compiler_params=params(3),
    )(
        length, rows, weights, qkv, att_t, lse, d_attended, out_part, small,
        hidden.reshape(seqs, 2, hs, width), gain.reshape(1, width), d_middle.reshape(seqs, 2, hs, width),
        gi_own, gi_sib, go_own, go_sib,
    )
    g_out = gout.reshape(2, width, half).transpose(1, 0, 2).reshape(width, width)
    g_pair = gpair.reshape(pairs, 2, 3, width, 128).transpose(2, 3, 1, 0, 4).reshape(3, width, width)
    return g_out, g_pair, sums, g_inner, g_outer, g_hidden.reshape(seqs, span, width)


def layer_norm(inputs, norm_gain, norm_shift):
    centered = inputs - jnp.mean(inputs, axis=-1, keepdims=True)
    variance = jnp.mean(centered * centered, axis=-1, keepdims=True)
    return centered * lax.rsqrt(variance + epsilon) * norm_gain + norm_shift


def on_device(
    hidden_in,
    cotangent,
    query_weight,
    key_weight,
    value_weight,
    output_weight,
    gain_one,
    shift_one,
    gain_two,
    shift_two,
    w_router,
    w_inner,
    w_outer,
    expert_ids,
    seq_lengths,
):
    seqs, span, width = hidden_in.shape
    tokens = seqs * span
    blocks = lax.axis_size("blk")
    columns = lax.axis_size("ep") // 2
    experts_n = w_router.shape[1]
    capacity = max(2, 2 * tokens // experts_n)
    slots = experts_n * capacity
    half = width // 2
    assert seqs * 2 == blocks and experts_n == columns
    z, e, c, base = place()

    inner_own = lax.all_gather(w_inner[0], "blk", axis=0)
    outer_own = lax.all_gather(w_outer[0], "blk", axis=0)
    flip = [(i, i ^ 1) for i in range(2 * columns)]
    inner_sib = lax.ppermute(inner_own, "ep", flip)
    outer_sib = lax.ppermute(outer_own, "ep", flip)

    inputs = hidden_in.astype(f32)
    normed = layer_norm(inputs, gain_one, shift_one).astype(bf16)

    token_experts = expert_ids.reshape(tokens)
    onehot = token_experts[:, None] == jnp.arange(experts_n, dtype=jnp.int32)[None, :]
    onehot_f = onehot.astype(f32)
    onehot_int = onehot.astype(jnp.int32)
    places = z * span + jnp.arange(span, dtype=jnp.int32)
    valid_rows = (places[None, :] < seq_lengths[:, None]).astype(f32).reshape(tokens)
    counts = lax.psum(jnp.sum(onehot_f * valid_rows[:, None], axis=0), ("blk", "ep"))
    mean_load = jnp.sum(counts) / experts_n
    load_ratio = (counts - mean_load) / mean_load
    slot_ranks = jnp.sum(jnp.cumsum(onehot_int, axis=0) * onehot_int, axis=1) - 1
    slot_rows = token_experts * capacity + slot_ranks
    to_slots = (jnp.arange(slots, dtype=jnp.int32)[:, None] == slot_rows[None, :]).astype(bf16)
    from_slots = (slot_rows[:, None] == jnp.arange(slots, dtype=jnp.int32)[None, :]).astype(bf16)

    column_lengths = lax.all_gather(seq_lengths, "ep")
    length = lax.dynamic_slice(
        column_lengths, (base + z // 2, lax.rem(z, 2)), (1, 1)
    ).reshape(1)

    def half_columns(weight):
        return lax.dynamic_slice_in_dim(weight, c * half, half, axis=1)

    w_qkv = jnp.concatenate(
        [half_columns(query_weight), half_columns(key_weight), half_columns(value_weight)], axis=1
    )

    rows_all = normed_exchange(normed, blocks)
    qkv, att, att_t, lse = attention_forward(length, rows_all, w_qkv, span)
    attended = attended_exchange(att, blocks)

    branch = jnp.einsum(
        "skqd,kde->sqe", attended, output_weight.reshape(2, half, width), preferred_element_type=f32
    )
    middle = (inputs + branch).reshape(tokens, width)
    normed_two_f, norm_two_pull = jax.vjp(layer_norm, middle, gain_two, shift_two)
    flat_rows = normed_two_f.astype(bf16)
    logits = jnp.dot(flat_rows, w_router, preferred_element_type=f32)
    gate_values = jax.nn.sigmoid(jnp.sum(logits * onehot_f, axis=1))
    scale_rows = valid_rows * gate_values
    grad_flat = cotangent.astype(f32).reshape(tokens, width)
    d_expert = (scale_rows[:, None] * grad_flat).astype(bf16)

    sent = jnp.dot(to_slots, jnp.concatenate([flat_rows, d_expert], axis=1), preferred_element_type=f32).astype(bf16)
    to_rows = sent[:, :width].reshape(columns, capacity, width)
    to_grads = sent[:, width:].reshape(columns, capacity, width)
    got_rows, got_grads = plane_exchange([to_rows, to_grads], columns, 7, "dispatch_exchange")
    produced, d_rows, gi_own, gi_sib, go_own, go_sib = experts(
        got_rows.reshape(-1, width),
        got_grads.reshape(-1, width),
        inner_own,
        inner_sib,
        outer_own,
        outer_sib,
    )
    back_rows, back_grads = plane_exchange(
        [
            produced.reshape(columns, capacity, width),
            d_rows.reshape(columns, capacity, width),
        ],
        columns,
        8,
        "return_exchange",
    )
    expert_out = jnp.dot(from_slots, back_rows.reshape(slots, width), preferred_element_type=f32)
    d_expert_rows = jnp.dot(from_slots, back_grads.reshape(slots, width), preferred_element_type=f32)

    output = (middle + scale_rows[:, None] * expert_out).reshape(seqs, span, width).astype(bf16)
    ratio_rows = jnp.sum(onehot_f * load_ratio[None, :], axis=1)
    local_balance = jnp.sum(scale_rows * ratio_rows)
    d_gate = valid_rows * (jnp.sum(grad_flat * expert_out, axis=1) + balance_weight * ratio_rows)
    d_logits = (onehot_f * (d_gate * gate_values * (1.0 - gate_values))[:, None]).astype(bf16)
    grad_router = jnp.einsum("td,te->ed", flat_rows, d_logits, preferred_element_type=f32)
    d_router_rows = jnp.einsum("te,de->td", d_logits, w_router, preferred_element_type=f32)
    d_middle_norm, grad_gain_two, grad_shift_two = norm_two_pull(d_expert_rows + d_router_rows)
    d_middle = (grad_flat + d_middle_norm).reshape(seqs, span, width)
    d_branch = d_middle.astype(bf16)
    out_part = jnp.einsum(
        "skqd,sqhe->hkde", attended, d_branch.reshape(seqs, span, 2, half), preferred_element_type=f32
    ).astype(bf16).reshape(2, width, half)
    d_attended = jnp.einsum(
        "sqe,kde->skqd", d_branch, output_weight.reshape(2, half, width), preferred_element_type=f32
    ).astype(bf16)
    vectors = jnp.concatenate(
        [
            jnp.zeros((2, width), f32),
            grad_gain_two[None],
            grad_shift_two[None],
            grad_router,
            jnp.full((1, width), local_balance, f32),
        ],
        axis=0,
    )
    vectors = jnp.pad(vectors, ((0, -vectors.shape[0] % 8), (0, 0)))
    g_out, g_qkv, sums, grad_inner, grad_outer, grad_hidden = backward(
        length, rows_all, w_qkv, qkv, att_t, lse, d_attended, out_part, vectors, hidden_in, gain_one, d_middle,
        gi_own, gi_sib, go_own, go_sib, span, columns,
    )
    dense = [g_qkv[0].astype(f32), g_qkv[1].astype(f32), g_qkv[2].astype(f32), g_out.astype(f32)]
    balance = sums[4 + experts_n, 0] / jnp.sum(counts)
    return (
        output,
        grad_hidden,
        dense[0],
        dense[1],
        dense[2],
        dense[3],
        sums[0],
        sums[1],
        sums[2],
        sums[3],
        jnp.transpose(sums[4 : 4 + experts_n]),
        grad_inner[None],
        grad_outer[None],
        balance,
    )


def solution(mesh):
    tokens = P("ep", "blk", None)
    return jax.shard_map(
        on_device,
        mesh=mesh,
        in_specs=(tokens, tokens)
        + (P(),) * 9
        + (P("ep", None, "blk"), P("ep", "blk", None), P("ep", "blk", None, None, None), P("ep")),
        out_specs=(tokens, tokens) + (P(),) * 9 + (P("ep", None, "blk"), P("ep", "blk", None), P()),
        check_vma=False,
    )
```

time: 630 us -> 594 us (0.943)
  Pallas kernels: 486 us -> 433 us
  local copies, waits for them, and re-layouts: 28.2 us -> 47.3 us
  other arithmetic: 32 us -> 23.9 us
    pallas_call x5 -> x1, Pallas kernels: 260 us -> 207 us  [backward(): pl.pallas_call(kernel, name='backward', out_shape=[jax.ShapeDtypeStruct((...]
    unnamed x103 -> x61, local copies, waits for them, and re-layouts: 15.1 us -> 23.3 us
  transfers between devices with their start and end apart: 4 -> 4, of which waited for: 0 -> 0; matrix products, arithmetic and copies ran while one was open for 5% -> 4% of each run, Pallas kernels for 24% -> 26%
where the time goes in v2:
time: 594 us; the launch traced here: 585 us
  Pallas kernels  433 us (73%)
  local copies, waits for them, and re-layouts  47.3 us (8%)
  blocking collectives  44.9 us (8%)
  other arithmetic  23.9 us (4%)
  between operations  18.5 us (3%)
  matrix products  14.8 us (2%)
    pallas_call x1, Pallas kernels, backward(): pl.pallas_call(kernel, name='backward', out_shape=[jax.ShapeDtypeStruct((...  207 us
    pallas_call x2, Pallas kernels, plane_exchange(): pl.pallas_call(kernel, name=name, out_shape=[jax.ShapeDtypeStruct(a.shape...  73.5 us
    pallas_call x1, Pallas kernels, normed_exchange(): pl.pallas_call(kernel, name='normed_exchange', out_shape=jax.ShapeDtypeSt...  59 us
    pallas_call x1, Pallas kernels, experts(): pl.pallas_call(kernel, name='experts', grid=(steps,), out_shape=[jax.Shap...  38.9 us
    psum x1, blocking collectives, on_device(): lax.psum(jnp.sum(onehot_f * valid_rows[:, None], axis=0), ('blk', 'ep'))  38.4 us
    pallas_call x1, Pallas kernels, attended_exchange(): pl.pallas_call(kernel, name='attended_exchange', out_shape=jax.ShapeDtype...  38 us
    unnamed x61, local copies, waits for them, and re-layouts  23.3 us
    pallas_call x1, Pallas kernels, attention_forward(): pl.pallas_call(kernel, name='attention_forward', out_shape=[jax.ShapeDtyp...  16.4 us
  transfers between devices with their start and end apart: 4, of which 0 were waited for; matrix products, arithmetic and copies ran while one was open for 4% of the time, Pallas kernels for 26%

profile of v2, /device:TPU:9, one launch (start us, length us, event | category | flops | bytes accessed | tf_op | source)
XLA Modules:
  0.0 584.5 jit_solution(4424819502047479387)
XLA Ops:
  7.3 0.7 all-gather.4.cloned.1.call-update
  8.0 0.7 all-gather.6.cloned.1.call-update
  8.7 1.2 dynamic-slice
  10.6 0.9 dynamic-update-slice
  11.6 6.5 %all-reduce.2 = s32[8,2]{1,0:T(8,128)S(1)} all-reduce(s32[8,2]{1,0:T(8,128)S(1)} %reshape.313), channel_id=2, replica_groups=mesh['blk'=4,'ep'=8] {'ep'}, use_global_device_ids=true, to_apply=%add.1 | all-reduce | flops 16 | bytes 128
  19.0 59.0 %normed_exchange.1 = bf16[4,2,128,768]{3,2,1,0:T(8,128)(2,1)S(1)} custom-call(bf16[2,2,128,768]{3,2,1,0:T(8,128)(2,1)S(1)} %bitcast.121), custom_call_target="tpu_custom_call" | custom-call | tf_op jit(solution)/shard_map/normed_exchange/pallas_call | solution.py:132
  78.1 2.5 constant_dynamic-slice_fusion.2
  80.6 2.2 constant_dynamic-slice_fusion
  82.8 2.8 pad_maximum_fusion.w_ref.refs_2_
  86.2 16.4 %attention_forward.1 = (bf16[1024,1152]{1,0:T(8,128)(2,1)}, bf16[4,256,384]{2,1,0:T(8,128)(2,1)S(1)}, f32[384,1024]{1,0:T(8,128)S(1)}, f32[6,1024]{1,0:T(8,128)S(1)}) custom-call(s32[1]{0:T(128)} %bitcast.1.len_ref.refs_0_, bf16[1024,768]{1,0:T(8,128)(2,1)S(1)} %bitcast.119, bf16[768,1152]{1,0:T(8,128)(2,1)} %pad_maximum_fusion.w_ref.refs_2_), custom_call_target="tpu_custom_call" | custom-call | flops 20000000000 | bytes 10000000 | tf_op jit(solution)/shard_map/attention_forward/pallas_call | solution.py:291
  102.6 1.1 copy-done.3
  104.3 38.0 %attended_exchange.1 = bf16[2,2,256,384]{3,2,1,0:T(8,128)(2,1)S(1)} custom-call(bf16[4,256,384]{2,1,0:T(8,128)(2,1)S(1)} %get-tuple-element.34.a_ref), custom_call_target="tpu_custom_call" | custom-call | tf_op jit(solution)/shard_map/attended_exchange/pallas_call | solution.py:190
  142.4 1.2 reduce-window.6
  144.2 1.9 fusion.41
  146.1 1.7 multiply_reduce_fusion.2
  148.5 38.4 %psum.7 = f32[4]{0:T(128)S(1)} all-reduce(f32[4]{0:T(128)S(1)} %select_reduce_fusion.1), channel_id=1, replica_groups=mesh['blk'=4,'ep'=8] {'blk','ep'}, use_global_device_ids=true, to_apply=%region_10.11 | all-reduce | flops 4 | bytes 32 | tf_op jit(solution)/shard_map/psum | solution.py:954
  188.4 1.8 add_convert_fusion
  191.4 1.8 convolution_convert_fusion
  193.2 1.9 fusion.40
  195.1 37.8 %dispatch_exchange.1 = (bf16[4,256,768]{2,1,0:T(8,128)(2,1)S(1)}, bf16[4,256,768]{2,1,0:T(8,128)(2,1)S(1)}) custom-call(bf16[4,256,768]{2,1,0:T(8,128)(2,1)} %bitcast.132, bf16[4,256,768]{2,1,0:T(8,128)(2,1)} %bitcast.131), custom_call_target="tpu_custom_call" | custom-call | tf_op jit(solution)/shard_map/dispatch_exchange/pallas_call | solution.py:224
  232.9 1.2 copy-done.10
  234.1 1.1 copy-done.11
  235.2 38.9 %experts.1 = (bf16[1024,768]{1,0:T(8,128)(2,1)S(1)}, bf16[1024,768]{1,0:T(8,128)(2,1)S(1)}, bf16[4,768,384]{2,1,0:T(8,128)(2,1)}, bf16[4,768,384]{2,1,0:T(8,128)...) custom-call(bf16[1024,768]{1,0:T(8,128)(2,1)} %bitcast.126, bf16[1024,768]{1,0:T(8,128)(2,1)} %bitcast.127, ...), custom_call_target="tpu_custom_call" | custom-call | flops 40000000000 | bytes 30000000 | tf_op jit(solution)/shard_map/experts/pallas_call | solution.py:359
  274.1 1.2 copy-done.4
  275.3 1.2 copy-done.5
  276.5 35.7 %return_exchange.1 = (bf16[4,256,768]{2,1,0:T(8,128)(2,1)S(1)}, bf16[4,256,768]{2,1,0:T(8,128)(2,1)S(1)}) custom-call(bf16[4,256,768]{2,1,0:T(8,128)(2,1)} %bitcast.122, bf16[4,256,768]{2,1,0:T(8,128)(2,1)} %bitcast.123), custom_call_target="tpu_custom_call" | custom-call | tf_op jit(solution)/shard_map/return_exchange/pallas_call | solution.py:224
  312.3 2.3 fusion.9
  315.2 3.9 multiply_reduce_fusion
  320.0 4.0 fusion.38
  324.0 1.7 fusion.37
  325.7 2.7 convert_element_type.111
  328.4 3.0 bitcast_convert_fusion
  331.5 0.8 fusion.15.refs_6_
  332.3 207.4 %backward.1 = (bf16[2,2,2,4,48,384]{5,4,3,2,1,0:T(8,128)(2,1)S(1)}, bf16[3,2,2,2,4,144,128]{6,5,4,3,2,1,0:T(8,128)(2,1)}, f32[16,768]{1,0:T(8,128)S(1)}, f32[768...) custom-call(s32[1]{0:T(128)} %bitcast.1.len_ref.refs_0_, bf16[1024,768]{1,0:T(8,128)(2,1)} %bitcast.120, ...), custom_call_target="tpu_custom_call" | custom-call | tf_op jit(solution)/shard_map/backward/pallas_call | solution.py:880
  539.7 1.0 copy-done.6
  542.5 6.0 %copy.44 = bf16[3,2,3,768,128]{3,4,0,1,2:T(8,128)(2,1)} copy(bf16[3,2,3,768,128]{4,3,2,1,0:T(8,128)(2,1)} %bitcast.133) | data formatting | bytes 7077888 | tf_op jit(solution)/shard_map/reshape | solution.py:901
  548.5 3.7 fusion.39
  552.1 1.7 bitcast_convert_fusion.3
  553.8 3.0 copy.46
  556.8 2.8 bitcast_convert_fusion.2
  559.7 3.0 copy.47
  562.7 2.8 bitcast_convert_fusion.1
  565.6 3.0 copy.48
  568.9 1.6 copy.58
  571.9 1.1 copy.71
  573.0 0.7 copy-done.7
  573.7 1.0 copy.72
  575.4 1.0 copy.73
  (97 shorter events, 9.6 us)
Async XLA Ops:
  7.2 137.0 %copy-start = (bf16[768,768]{1,0:T(8,128)(2,1)S(1)}, bf16[768,768]{1,0:T(8,128)(2,1)}, u32[]{:S(2)}) copy-start(bf16[768,768]{1,0:T(8,128)(2,1)} %param.20) | copy-start | bytes 3538948
  7.2 10.9 %copy-start.1 = (bf16[2,256,768]{2,1,0:T(8,128)(2,1)S(1)}, bf16[2,256,768]{2,1,0:T(8,128)(2,1)}, u32[]{:S(2)}) copy-start(bf16[2,256,768]{2,1,0:T(8,128)(2,1)} %param.15) | copy-start | bytes 2359300
  7.2 11.4 %copy-start.21 = (f32[768]{0:T(1024)S(1)}, f32[768]{0:T(1024)}, u32[]{:S(2)}) copy-start(f32[768]{0:T(1024)} %param.21) | copy-start | bytes 9220
  7.2 11.4 %copy-start.22 = (f32[768]{0:T(1024)S(1)}, f32[768]{0:T(1024)}, u32[]{:S(2)}) copy-start(f32[768]{0:T(1024)} %param.22) | copy-start | bytes 9220
  7.2 140.7 %all-gather.4.cloned.1.call-start = ((), (), s32[]{:S(2)}) async-start(), calls=%async_computation | async-start | bytes 2949120 | tf_op jit(solution)/shard_map/all_gather | solution.py:939
  8.0 140.0 %all-gather.6.cloned.1.call-start = ((), (), s32[]{:S(2)}) async-start(), calls=%async_computation.1 | async-start | bytes 2949120 | tf_op jit(solution)/shard_map/all_gather | solution.py:940
  78.1 8.1 %copy-start.2 = (bf16[4,2,128,768]{3,2,1,0:T(8,128)(2,1)}, bf16[4,2,128,768]{3,2,1,0:T(8,128)(2,1)S(1)}, u32[]{:S(2)}) copy-start(bf16[4,2,128,768]{3,2,1,0:T(8,128)(2,1)S(1)} %normed_exchange.1) | copy-start | bytes 4718596
  78.1 2.5 copy-start.17
  102.6 1.1 copy-start.3
  103.7 0.6 copy-start.8
  104.3 38.0 %copy-start.24 = (s32[2]{0:T(128)S(1)}, s32[2]{0:T(128)}, u32[]{:S(2)}) copy-start(s32[2]{0:T(128)} %param.29) | copy-start | bytes 28
  104.3 38.1 %copy-start.18 = (s32[1,1,2,256,1]{3,4,2,1,0:T(1,128)S(1)}, s32[1,1,2,256,1]{3,4,2,1,0:T(1,128)}, u32[]{:S(2)}) copy-start(s32[1,1,2,256,1]{3,4,2,1,0:T(1,128)} %param.28) | copy-start | bytes 6148
  146.1 42.3 %copy-start.20 = (f32[768]{0:T(1024)S(1)}, f32[768]{0:T(1024)}, u32[]{:S(2)}) copy-start(f32[768]{0:T(1024)} %param.23) | copy-start | bytes 9220
  146.1 42.3 %copy-start.23 = (f32[768]{0:T(1024)S(1)}, f32[768]{0:T(1024)}, u32[]{:S(2)}) copy-start(f32[768]{0:T(1024)} %param.24) | copy-start | bytes 9220
  147.8 42.4 %copy-start.19 = (bf16[768,4]{0,1:T(4,128)(2,1)S(1)}, bf16[768,4]{0,1:T(4,128)(2,1)}, u32[]{:S(2)}) copy-start(bf16[768,4]{0,1:T(4,128)(2,1)} %param.25) | copy-start | bytes 18436
  147.9 87.3 %collective-permute-start = (bf16[4,768,384]{2,1,0:T(8,128)(2,1)}, bf16[4,768,384]{2,1,0:T(8,128)(2,1)}, u32[]{:S(2)}, u32[]{:S(2)}) collective-permute-start(bf16[4,768,384]{2,1,0:T(8,128)(2,1)} %all-gather.4.cloned.1.call-done.io_ref), channel_id=1, source_target_pairs={{0,1},{1,0},{2,3},{3,2},{4,5},{5,4},{6,7},{7,6},{8,9},{9,8},{10,11... | collective-permute-start | bytes 7077896 | tf_op jit(solution)/shard_map/ppermute | solution.py:942
  148.0 87.2 %collective-permute-start.1 = (bf16[4,384,768]{2,1,0:T(8,128)(2,1)}, bf16[4,384,768]{2,1,0:T(8,128)(2,1)}, u32[]{:S(2)}, u32[]{:S(2)}) collective-permute-start(bf16[4,384,768]{2,1,0:T(8,128)(2,1)} %all-gather.6.cloned.1.call-done.oo_ref), channel_id=1, source_target_pairs={{0,1},{1,0},{2,3},{3,2},{4,5},{5,4},{6,7},{7,6},{8,9},{9,8},{10,11... | collective-permute-start | bytes 7077896 | tf_op jit(solution)/shard_map/ppermute | solution.py:943
  188.4 2.8 copy-start.12
  232.9 1.2 copy-start.10
  234.1 1.1 copy-start.11
  274.1 1.2 copy-start.4
  275.3 1.2 copy-start.5
  319.9 4.0 copy-start.13
  328.4 3.1 copy-start.14
  331.5 0.8 copy-start.9
  539.7 1.0 copy-start.6
  568.9 3.0 copy-start.15
  571.9 1.8 copy-start.7
  573.7 1.7 copy-start.16
Sparse Core Ops, SparseCore 0:
  9.6 64.6 all-gather.3
  75.9 65.7 all-gather.5
